TPU v7x, 256 devices: a whole 4x4x8 slice. The times are simulated.
256 devices in a mesh: dp: 4 (over y), expert: 64 (over x, z, core).
Axes of the slice: x: 4, y: 4, z: 8, core: 2. Of those that a mesh axis runs over, the one named last changes fastest.
Arguments:
- tokens: bfloat16 [32768, 2048], P(('dp', 'expert')), may hold values from -24 to 24
- routes: int32 [32768, 8], P(('dp', 'expert')), may hold values from 0 to 63, all different within a row; in each aligned block of 128 rows (0 to 127, 128 to 255, ...) at most 20 rows name the same one
- gate_values: float32 [32768, 8], P(('dp', 'expert')), may hold values from 0.05 to 1
- latent_down: bfloat16 [2048, 512], replicated, may hold values from -0.125 to 0.125
- gate_weight: bfloat16 [64, 512, 1024], P('expert'), may hold values from -0.25 to 0.25
- up_weight: bfloat16 [64, 512, 1024], P('expert'), may hold values from -0.25 to 0.25
- out_weight: bfloat16 [64, 1024, 512], P('expert'), may hold values from -0.1875 to 0.1875
- latent_up: bfloat16 [2048, 512], replicated, may hold values from -0.25 to 0.25
- grad_mixed: bfloat16 [32768, 2048], P(('dp', 'expert')), may hold values from -24 to 24
Outputs:
- mixed: bfloat16 [32768, 2048], P(('dp', 'expert'))
- grad_tokens: bfloat16 [32768, 2048], P(('dp', 'expert'))
- grad_latent_down: float32 [2048, 512], P('expert')
- grad_latent_up: float32 [2048, 512], P('expert')
- grad_gate_weight: float32 [64, 512, 1024], P('expert', None, 'dp')
- grad_up_weight: float32 [64, 512, 1024], P('expert', None, 'dp')
- grad_out_weight: float32 [64, 1024, 512], P('expert', 'dp')
Inputs may be any that keep to these rules, and one draw needn't show every extreme that they name: `routes`: each row names 8 different experts. Within the 128 rows of one device no expert is named by more than 20 rows, a bound that some block reaches.
All inputs are finite; a program needn't handle non-finite values.
Results may differ from a plain program's by a relative error of at most 0.02.
Values may be sent and summed in bfloat16 or wider, within the bound.
A program may use at most 128 MiB of HBM per device.

v0:
```python
from functools import partial

import jax
import jax.numpy as jnp
from jax import lax
from jax.sharding import PartitionSpec as P

CONTRACT_ROWS = (((0,), (0,)), ((), ()))
CONTRACT_COLS = (((1,), (1,)), ((), ()))


def flatten_rows(values):
    return values.reshape(-1, values.shape[-1])


def expert_rows(gate_matrix, up_matrix, out_matrix, inputs):
    latent_in, grad_in = inputs
    sources, slot_count, latent_width = latent_in.shape
    hidden = gate_matrix.shape[1]
    rows_in = latent_in.reshape(sources * slot_count, latent_width)
    grad_rows = grad_in.reshape(sources * slot_count, latent_width)
    pre_gate = jnp.dot(rows_in, gate_matrix, preferred_element_type=jnp.float32)
    pre_up = jnp.dot(rows_in, up_matrix, preferred_element_type=jnp.float32)
    sigmoid_gate = jax.nn.sigmoid(pre_gate)
    swish_gate = pre_gate * sigmoid_gate
    activation = (swish_gate * pre_up).astype(jnp.bfloat16)
    expert_out = jnp.dot(activation, out_matrix, preferred_element_type=jnp.float32).astype(
        jnp.bfloat16
    )
    grad_act = lax.dot_general(
        grad_rows, out_matrix, CONTRACT_COLS, preferred_element_type=jnp.float32
    )
    grad_gate = (grad_act * pre_up * sigmoid_gate * (1.0 + pre_gate * (1.0 - sigmoid_gate))).astype(
        jnp.bfloat16
    )
    grad_up = (grad_act * swish_gate).astype(jnp.bfloat16)
    grad_back = lax.dot_general(
        grad_gate, gate_matrix, CONTRACT_COLS, preferred_element_type=jnp.float32
    )
    grad_back = grad_back + lax.dot_general(
        grad_up, up_matrix, CONTRACT_COLS, preferred_element_type=jnp.float32
    )
    grad_back = grad_back.astype(jnp.bfloat16)
    shape_latent = (sources, slot_count, latent_width)
    shape_hidden = (sources, slot_count, hidden)
    returned_out, returned_grad = (
        lax.all_to_all(
            expert_out.reshape(shape_latent), "expert", split_axis=0, concat_axis=0, tiled=True
        ),
        lax.all_to_all(
            grad_back.reshape(shape_latent), "expert", split_axis=0, concat_axis=0, tiled=True
        ),
    )
    return (
        returned_out,
        returned_grad,
        activation.reshape(shape_hidden),
        grad_gate.reshape(shape_hidden),
        grad_up.reshape(shape_hidden),
        latent_in,
        grad_in,
    )


def term_rows(token_cols, cotan_cols, grad_latent, combined, start_row, row_count):
    down_term = lax.dot_general(
        token_cols, grad_latent, CONTRACT_ROWS, preferred_element_type=jnp.float32
    )
    up_term = lax.dot_general(
        cotan_cols, combined, CONTRACT_ROWS, preferred_element_type=jnp.float32
    )
    return jnp.concatenate([down_term, up_term], axis=1)


def shards(
    tokens,
    routes,
    gate_values,
    latent_down,
    gate_weight,
    up_weight,
    out_weight,
    latent_up,
    grad_mixed,
):
    token_count, route_count = routes.shape
    expert_count = lax.axis_size("expert")
    latent_width = latent_down.shape[1]
    feature_count = tokens.shape[1]
    capacity = min(token_count, 5 * token_count * route_count // (4 * expert_count))
    latent = jnp.dot(tokens, latent_down, preferred_element_type=jnp.float32).astype(jnp.bfloat16)
    grad_comb = jnp.dot(grad_mixed, latent_up, preferred_element_type=jnp.float32)
    flat_routes = routes.reshape(-1)
    onehot = (flat_routes[:, None] == jnp.arange(expert_count, dtype=jnp.int32)[None, :]).astype(
        jnp.int32
    )
    before = jnp.cumsum(onehot, axis=0, dtype=jnp.int32) - onehot
    slot_index = jnp.sum(before * onehot, axis=1, dtype=jnp.int32)
    slot_place = flat_routes * capacity + slot_index
    row_ids = jnp.arange(token_count * route_count, dtype=jnp.int32) + 1
    slot_owner = jnp.zeros((expert_count * capacity,), jnp.int32).at[slot_place].set(row_ids)
    filled = (slot_owner > 0)[:, None]
    source_row = jnp.maximum(slot_owner - 1, 0)
    token_row = source_row // route_count
    flat_gates = gate_values.reshape(-1)
    send_latent = jnp.where(
        filled, jnp.take(latent, token_row, axis=0), jnp.zeros((), jnp.bfloat16)
    )
    scaled = (
        jnp.take(flat_gates, source_row)[:, None] * jnp.take(grad_comb, token_row, axis=0)
    ).astype(jnp.bfloat16)
    send_grad = jnp.where(filled, scaled, jnp.zeros((), jnp.bfloat16))
    send_shape = (expert_count, capacity, latent_width)
    run_expert = partial(expert_rows, gate_weight[0], up_weight[0], out_weight[0])
    results = run_expert(
        (
            lax.all_to_all(
                send_latent.reshape(send_shape), "expert", split_axis=0, concat_axis=0, tiled=True
            ),
            lax.all_to_all(
                send_grad.reshape(send_shape), "expert", split_axis=0, concat_axis=0, tiled=True
            ),
        )
    )
    back_out, back_grad, activation, grad_gate, grad_up, recv_latent, recv_grad = results
    picked_out = jnp.take(flatten_rows(back_out), slot_place, axis=0).reshape(
        token_count, route_count, latent_width
    )
    combined = jnp.sum(picked_out.astype(jnp.float32) * gate_values[:, :, None], axis=1).astype(
        jnp.bfloat16
    )
    picked_grad = jnp.take(flatten_rows(back_grad), slot_place, axis=0).reshape(
        token_count, route_count, latent_width
    )
    grad_latent = jnp.sum(picked_grad.astype(jnp.float32), axis=1).astype(jnp.bfloat16)
    mixed = lax.dot_general(
        combined, latent_up, CONTRACT_COLS, preferred_element_type=jnp.float32
    ).astype(jnp.bfloat16)
    grad_tokens = lax.dot_general(
        grad_latent, latent_down, CONTRACT_COLS, preferred_element_type=jnp.float32
    ).astype(jnp.bfloat16)
    grad_gate_part = lax.dot_general(
        flatten_rows(recv_latent),
        flatten_rows(grad_gate),
        CONTRACT_ROWS,
        preferred_element_type=jnp.float32,
    )
    grad_up_part = lax.dot_general(
        flatten_rows(recv_latent),
        flatten_rows(grad_up),
        CONTRACT_ROWS,
        preferred_element_type=jnp.float32,
    )
    grad_out_part = lax.dot_general(
        flatten_rows(activation),
        flatten_rows(recv_grad),
        CONTRACT_ROWS,
        preferred_element_type=jnp.float32,
    )
    gate_total, up_total, out_total = (
        lax.psum_scatter(
            grad_gate_part.astype(jnp.bfloat16), "dp", scatter_dimension=1, tiled=True
        ).astype(jnp.float32),
        lax.psum_scatter(
            grad_up_part.astype(jnp.bfloat16), "dp", scatter_dimension=1, tiled=True
        ).astype(jnp.float32),
        lax.psum_scatter(
            grad_out_part.astype(jnp.bfloat16), "dp", scatter_dimension=0, tiled=True
        ).astype(jnp.float32),
    )
    term_fn = partial(term_rows, tokens, grad_mixed, grad_latent, combined)
    partial_terms = lax.psum_scatter(
        term_fn(jnp.int32(0), lax.axis_size("expert") * (feature_count // expert_count)),
        "expert",
        scatter_dimension=0,
        tiled=True,
    )
    proj_grads = lax.psum(partial_terms.astype(jnp.bfloat16), "dp").astype(jnp.float32)
    return (
        mixed,
        grad_tokens,
        proj_grads[:, :latent_width],
        proj_grads[:, latent_width:],
        gate_total[None],
        up_total[None],
        out_total[None],
    )


def solution(mesh):
    in_specs = (
        P(("dp", "expert"), None),
        P(("dp", "expert"), None),
        P(("dp", "expert"), None),
        P(),
        P("expert", None, None),
        P("expert", None, None),
        P("expert", None, None),
        P(),
        P(("dp", "expert"), None),
    )
    out_specs = (
        P(("dp", "expert"), None),
        P(("dp", "expert"), None),
        P("expert", None),
        P("expert", None),
        P("expert", None, "dp"),
        P("expert", None, "dp"),
        P("expert", "dp", None),
    )
    return jax.shard_map(shards, mesh=mesh, in_specs=in_specs, out_specs=out_specs, check_vma=False)
```

profile of v0, /device:TPU:1, one launch (start us, length us, event | category | flops | bytes accessed | tf_op | source)
XLA Modules:
  0.0 500.8 jit_solution(6227542150012333032)
XLA Ops:
  9.2 18.0 %reduce-window.6 = s32[64,8,128]{2,1,0:T(8,128)S(1)} reduce-window(s32[64,8,128]{2,1,0:T(8,128)S(1)} %fusion.17, s32[]{:T(128)} %constant.77.clone.1), window={size=1x1x128 pad=0_0x0_0x127_0}, to_apply=%region_0.0 | reduce-window | flops 8323072 | bytes 524292 | tf_op jit(solution)/shard_map/reduce-window
  27.9 4.3 scatter_custom_fusion
  32.5 5.0 gather_fusion.1
  40.1 4.1 gather_fusion
  47.8 4.4 gather_fusion.2
  52.2 3.9 gather.23
  56.2 3.6 fusion.3
  59.8 52.7 %all_to_all.20 = bf16[64,20,512]{2,1,0:T(8,128)(2,1)} all-to-all(bf16[64,20,512]{2,1,0:T(8,128)(2,1)S(1)} %get-tuple-element.37), channel_id=1, replica_groups=mesh['dp'=4,'expert'=64] {'expert'}, dimensions={0} | all-to-all | bytes 2621440 | tf_op jit(solution)/shard_map/all_to_all | solution.py:117
  112.5 6.3 %all-to-all-start.2 = ((bf16[64,20,512]{2,1,0:T(8,128)(2,1)}), bf16[64,20,512]{2,1,0:T(8,128)(2,1)}, u32[]{:S(2)}, u32[]{:S(2)}) async-start(bf16[64,20,512]{2,1,0:T(8,128)(2,1)} %get-tuple-element.36), calls=%async_computation.2 | async-start | bytes 3145728 | tf_op jit(solution)/shard_map/all_to_all | solution.py:120
  121.1 5.2 %fusion.8 = f32[1280,1024]{1,0:T(8,128)} fusion(bf16[1280,512]{1,0:T(8,128)(2,1)S(1)} %reshape.137, bf16[1,512,1024]{2,1,0:T(8,128)(2,1)} %param.16), kind=kOutput, calls=%fused_computation.33 | convolution fusion | flops 1342177280 | bytes 7602176 | tf_op jit(solution)/shard_map/dot_general | solution.py:23
  126.3 3.8 fusion.12
  130.1 28.4 %all-to-all-done.2 = bf16[64,20,512]{2,1,0:T(8,128)(2,1)} async-done(((bf16[64,20,512]{2,1,0:T(8,128)(2,1)}), bf16[64,20,512]{2,1,0:T(8,128)(2,1)}, u32[]{:S(2)}, u32[]{:S(2)}) %all-to-all-start.2) | async-done | bytes 1310752 | tf_op jit(solution)/shard_map/all_to_all | solution.py:120
  158.5 3.3 reshape.141
  161.8 9.8 %multiply_convert_fusion = (bf16[1280,1024]{1,0:T(8,128)(2,1)S(1)}, bf16[1280,1024]{1,0:T(8,128)(2,1)S(1)}, bf16[1280,1024]{1,0:T(8,128)(2,1)}) fusion(f32[1280,1024]{1,0:T(8,128)} %fusion.12, f32[1280,1024]{1,0:T(8,128)} %fusion.8, bf16[1280,512]{1,0:T(8,128)(2,1)} %reshape.141, bf16[1,1024,512]{2,1,0:T(8,128)(2,1)} %param.17), kind=kOutput, calls=%fused_computation.7 | convolution fusion | flops 1361838080 | bytes 20709376 | tf_op jit(solution)/shard_map/dot_general | solution.py:30
  173.8 2.7 fusion.1
  176.6 3.2 reshape.142
  179.8 6.3 %all-to-all-start.3 = ((bf16[64,20,512]{2,1,0:T(8,128)(2,1)}), bf16[64,20,512]{2,1,0:T(8,128)(2,1)}, u32[]{:S(2)}, u32[]{:S(2)}) async-start(bf16[64,20,512]{2,1,0:T(8,128)(2,1)} %reshape.142), calls=%async_computation.3 | async-start | bytes 3145728 | tf_op jit(solution)/shard_map/all_to_all | solution.py:50
  186.1 4.6 convolution_convert_fusion.3
  191.1 4.3 convolution_convert_fusion.4
  195.4 4.7 convolution_convert_fusion
  200.0 3.2 reshape.138
  203.2 22.6 %all-to-all-done.3 = bf16[64,20,512]{2,1,0:T(8,128)(2,1)} async-done(((bf16[64,20,512]{2,1,0:T(8,128)(2,1)}), bf16[64,20,512]{2,1,0:T(8,128)(2,1)}, u32[]{:S(2)}, u32[]{:S(2)}) %all-to-all-start.3) | async-done | bytes 1310752 | tf_op jit(solution)/shard_map/all_to_all | solution.py:50
  225.8 6.3 %all-to-all-start.1 = ((bf16[64,20,512]{2,1,0:T(8,128)(2,1)}), bf16[64,20,512]{2,1,0:T(8,128)(2,1)}, u32[]{:S(2)}, u32[]{:S(2)}) async-start(bf16[64,20,512]{2,1,0:T(8,128)(2,1)} %reshape.138), calls=%async_computation.1 | async-start | bytes 3145728 | tf_op jit(solution)/shard_map/all_to_all | solution.py:47
  232.2 4.3 convolution_convert_fusion.5
  238.8 5.1 %gather_fusion.4 = bf16[1024,512]{1,0:T(8,128)(2,1)} fusion(bf16[1280,512]{1,0:T(8,128)(2,1)S(1)} %reshape.143, s32[1024]{0:T(1024)S(1)} %broadcast_clamp_fusion), kind=kCustom, calls=%fused_computation.1.clone | custom fusion | bytes 2101248 | tf_op jit(solution)/shard_map/jit(_take)/gather | solution.py:132
  243.9 27.9 %all-to-all-done.1 = bf16[64,20,512]{2,1,0:T(8,128)(2,1)} async-done(((bf16[64,20,512]{2,1,0:T(8,128)(2,1)}), bf16[64,20,512]{2,1,0:T(8,128)(2,1)}, u32[]{:S(2)}, u32[]{:S(2)}) %all-to-all-start.1) | async-done | bytes 1310752 | tf_op jit(solution)/shard_map/all_to_all | solution.py:47
  274.1 5.1 %gather_fusion.3 = bf16[1024,512]{1,0:T(8,128)(2,1)} fusion(bf16[1280,512]{1,0:T(8,128)(2,1)S(1)} %reshape.139, s32[1024]{0:T(1024)S(1)} %broadcast_clamp_fusion), kind=kCustom, calls=%fused_computation.clone | custom fusion | bytes 2101248 | tf_op jit(solution)/shard_map/jit(_take)/gather | solution.py:126
  285.0 3.8 pad_maximum_fusion
  288.8 9.3 %copy.37 = f32[2048,1024]{1,0:T(8,128)} copy(f32[2048,1024]{0,1:T(8,128)} %pad_maximum_fusion) | data formatting | bytes 16777216
  305.1 136.4 %reduce-scatter.13.cloned.1.call-done = f32[32,1024]{1,0:T(8,128)} async-done(((f32[2048,1024]{1,0:T(8,128)}), f32[32,1024]{1,0:T(8,128)}) %reduce-scatter.13.cloned.1.call-update) | async-done | bytes 131088
  443.3 3.2 convolution_convert_fusion.2
  446.5 45.3 %all-reduce.2.cloned.1.call-done = bf16[32,1024]{0,1:T(8,128)(2,1)} async-done(((bf16[32,1024]{0,1:T(8,128)(2,1)}), bf16[32,1024]{0,1:T(8,128)(2,1)}) %all-reduce.2.cloned.1.call-update) | async-done | bytes 65552 | tf_op jit(solution)/shard_map/psum | solution.py:178
  (90 shorter events, 35.6 us)
Async XLA Ops:
  7.2 32.5 %copy-start = (bf16[2048,512]{1,0:T(8,128)(2,1)S(1)}, bf16[2048,512]{1,0:T(8,128)(2,1)}, u32[]{:S(2)}) copy-start(bf16[2048,512]{1,0:T(8,128)(2,1)} %param.14) | copy-start | bytes 6291460
  7.2 25.1 %copy-start.11 = (f32[128,8]{0,1:T(8,128)S(1)}, f32[128,8]{0,1:T(8,128)}, u32[]{:S(2)}) copy-start(f32[128,8]{0,1:T(8,128)} %param.13) | copy-start | bytes 12292
  32.4 5.1 %copy-start.6 = (f32[128,8]{1,0:T(8,128)}, f32[128,8]{1,0:T(8,128)S(1)}, u32[]{:S(2)}) copy-start(f32[128,8]{1,0:T(8,128)S(1)} %copy.33) | copy-start | bytes 12292
  32.5 7.2 %copy-start.4 = (bf16[128,2048]{1,0:T(8,128)(2,1)S(1)}, bf16[128,2048]{1,0:T(8,128)(2,1)}, u32[]{:S(2)}) copy-start(bf16[128,2048]{1,0:T(8,128)(2,1)} %param.11) | copy-start | bytes 1572868
  52.2 3.9 copy-start.8
  52.2 4.0 copy-start.9
  52.2 4.0 copy-start.10
  112.5 46.0 %all-to-all-start.2 = ((bf16[64,20,512]{2,1,0:T(8,128)(2,1)}), bf16[64,20,512]{2,1,0:T(8,128)(2,1)}, u32[]{:S(2)}, u32[]{:S(2)}) async-start(bf16[64,20,512]{2,1,0:T(8,128)(2,1)} %get-tuple-element.36), calls=%async_computation.2 | async-start | bytes 3145728 | tf_op jit(solution)/shard_map/all_to_all | solution.py:120
  121.1 5.2 %copy-start.12 = (bf16[1,512,1024]{2,1,0:T(8,128)(2,1)S(1)}, bf16[1,512,1024]{2,1,0:T(8,128)(2,1)}, u32[]{:S(2)}) copy-start(bf16[1,512,1024]{2,1,0:T(8,128)(2,1)} %param.15) | copy-start | bytes 3145732
  161.8 9.8 %copy-start.13 = (bf16[1,512,1024]{2,1,0:T(8,128)(2,1)S(1)}, bf16[1,512,1024]{2,1,0:T(8,128)(2,1)}, u32[]{:S(2)}) copy-start(bf16[1,512,1024]{2,1,0:T(8,128)(2,1)} %param.15) | copy-start | bytes 3145732
  171.5 1.6 copy-start.1
  171.6 2.3 copy-start.2
  171.6 2.3 copy-start.14
  179.8 46.0 %all-to-all-start.3 = ((bf16[64,20,512]{2,1,0:T(8,128)(2,1)}), bf16[64,20,512]{2,1,0:T(8,128)(2,1)}, u32[]{:S(2)}, u32[]{:S(2)}) async-start(bf16[64,20,512]{2,1,0:T(8,128)(2,1)} %reshape.142), calls=%async_computation.3 | async-start | bytes 3145728 | tf_op jit(solution)/shard_map/all_to_all | solution.py:50
  186.1 112.1 %reduce-scatter.11.cloned.1.call-start = ((), (), s32[]{:S(2)}) async-start(), calls=%async_computation.11 | async-start | bytes 1310720 | tf_op jit(solution)/shard_map/reduce_scatter | solution.py:167
  190.8 109.2 %reduce-scatter.9.cloned.1.call-start = ((), (), s32[]{:S(2)}) async-start(), calls=%async_computation.10 | async-start | bytes 1310720 | tf_op jit(solution)/shard_map/reduce_scatter | solution.py:164
  225.8 46.0 %all-to-all-start.1 = ((bf16[64,20,512]{2,1,0:T(8,128)(2,1)}), bf16[64,20,512]{2,1,0:T(8,128)(2,1)}, u32[]{:S(2)}, u32[]{:S(2)}) async-start(bf16[64,20,512]{2,1,0:T(8,128)(2,1)} %reshape.138), calls=%async_computation.1 | async-start | bytes 3145728 | tf_op jit(solution)/shard_map/all_to_all | solution.py:47
  232.1 69.7 %reduce-scatter.7.cloned.1.call-start = ((), (), s32[]{:S(2)}) async-start(), calls=%async_computation.9 | async-start | bytes 1310720 | tf_op jit(solution)/shard_map/reduce_scatter | solution.py:161
  236.5 205.1 %reduce-scatter.13.cloned.1.call-start = ((), (), s32[]{:S(2)}) async-start(), calls=%async_computation.12 | async-start | bytes 8519680
  274.1 7.0 %copy-start.7 = (f32[128,8]{1,0:T(8,128)S(1)}, f32[128,8]{1,0:T(8,128)}, u32[]{:S(2)}) copy-start(f32[128,8]{1,0:T(8,128)} %copy-done.6) | copy-start | bytes 12292
  279.3 3.9 copy-start.3
  283.2 1.0 copy-start.5
  298.1 193.7 %all-reduce.2.cloned.1.call-start = ((), (), s32[]{:S(2)}) async-start(), calls=%async_computation.8 | async-start | bytes 524288 | tf_op jit(solution)/shard_map/psum | solution.py:178
Sparse Core Ops, SparseCore 0:
  190.9 25.6 reduce-scatter.10
  219.3 26.0 reduce-scatter.8
  247.9 25.7 reduce-scatter.6
  298.2 143.2 reduce-scatter.12
  443.7 48.0 all-reduce.1
where the time goes:
time: 503 us; the launch traced here: 501 us
  waiting for transfers between devices  261 us (52%)
  local copies, waits for them, and re-layouts  68.3 us (14%)
  blocking collectives  52.7 us (10%)
  matrix products  49.8 us (10%)
  other arithmetic  35.9 us (7%)
  starting transfers between devices  19.3 us (4%)
  between operations  14.1 us (3%)
    unnamed x6, waiting for transfers between devices  136 us
    all_to_all x1, blocking collectives, shards(): lax.all_to_all(send_latent.reshape(send_shape), 'expert', split_axis=0, c...  52.7 us
    psum x1, waiting for transfers between devices, shards(): lax.psum(partial_terms.astype(jnp.bfloat16), 'dp').astype(jnp.float32)  45.3 us
    all_to_all x1, waiting for transfers between devices, shards(): lax.all_to_all(send_grad.reshape(send_shape), 'expert', split_axis=0, con...  28.4 us
    all_to_all x1, waiting for transfers between devices, expert_rows(): lax.all_to_all(expert_out.reshape(shape_latent), 'expert', split_axis=0,...  27.9 us
    all_to_all x1, waiting for transfers between devices, expert_rows(): lax.all_to_all(grad_back.reshape(shape_latent), 'expert', split_axis=0, c...  22.6 us
    another operation x3, other arithmetic  18.2 us
    unnamed x36, local copies, waits for them, and re-layouts  14.4 us
  transfers between devices with their start and end apart: 8, of which 5 were waited for; matrix products, arithmetic and copies ran while one was open for 15% of the time, Pallas kernels for 0%

commit v1 on v0

v1 whole, which is shorter than its diff:
```python
from functools import partial

import jax
import jax.numpy as jnp
from jax import lax
from jax.experimental import pallas as pl
from jax.experimental.pallas import tpu as pltpu
from jax.sharding import PartitionSpec as P

MESH = pl.DeviceIdType.MESH
ROWS = (((0,), (0,)), ((), ()))
COLS = (((1,), (1,)), ((), ()))
PLAIN = (((1,), (0,)), ((), ()))
F32 = jnp.float32
BF16 = jnp.bfloat16

RING = 8
CORES = 2
CAP = 20
MAIN = 16
EXTRA = 4
SET = 4
SET_ROWS = SET * CAP


def dot(a, b, dims=PLAIN):
    return lax.dot_general(a, b, dims, preferred_element_type=F32)


def layer_kernel(
    ring,
    routes_ref,
    gates_ref,
    tokens_ref,
    cotan_ref,
    down_ref,
    up_ref,
    gw_ref,
    uw_ref,
    ow_ref,
    mid_ref,
    gate_grad_ref,
    up_grad_ref,
    out_grad_ref,
    gathered,
    send_rows,
    expert_rows,
    result_rows,
    back_rows,
    pick,
    weigh,
    extra_sum,
    act,
    grad_gate,
    grad_up,
    ring_out,
    ring_in,
    grads_out,
    grads_in,
    gather_send,
    gather_recv,
    slot_send,
    slot_recv,
    back_send,
    back_recv,
    own_sem,
    ring_send,
    ring_recv,
    grad_send,
    grad_recv,
):
    tokens_here, latent = tokens_ref.shape[0], down_ref.shape[1]
    hidden = gw_ref.shape[1]
    experts = lax.axis_size("expert")
    groups = lax.axis_size("dp")
    columns = experts // (ring * CORES)
    peers = columns * CORES
    half = ring // 2
    sets = ring // SET
    me = lax.axis_index("expert")
    my_group = lax.axis_index("dp")
    z = lax.rem(lax.div(me, CORES), ring)
    core = lax.rem(me, CORES)
    place = lax.div(me, ring * CORES) * CORES + core

    def on_ring(step):
        other = lax.rem(z + step + ring, ring)
        return (my_group, me + (other - z) * CORES)

    def at_peer(d):
        return (my_group, (lax.div(d, CORES) * ring + z) * CORES + lax.rem(d, CORES))

    def peer(j):
        return lax.rem(place + j, peers)

    def group_at(k):
        return (lax.rem(my_group + k, groups), me)

    barrier = pltpu.get_barrier_semaphore()
    for step in (1, -1):
        pl.semaphore_signal(barrier, inc=1, device_id=on_ring(step), device_id_type=MESH)
    for j in range(1, peers):
        pl.semaphore_signal(barrier, inc=1, device_id=at_peer(peer(j)), device_id_type=MESH)
    for k in range(1, groups):
        pl.semaphore_signal(barrier, inc=1, device_id=group_at(k), device_id_type=MESH)

    gathered[0, 0:tokens_here, 0:latent] = dot(tokens_ref[...], down_ref[...]).astype(BF16)
    gathered[0, 0:tokens_here, latent:] = dot(cotan_ref[...], up_ref[...]).astype(BF16)
    expert_ids = lax.broadcasted_iota(jnp.int32, (experts, tokens_here), 0)
    table = jnp.zeros((experts, tokens_here), F32)
    for k in range(routes_ref.shape[0]):
        table = table + jnp.where(expert_ids == routes_ref[k : k + 1, :], gates_ref[k : k + 1, :], 0.0)
    table_high = table.astype(BF16)
    table_low = (table - table_high.astype(F32)).astype(BF16)
    per_column = ring * CORES
    for b in range(columns):
        rows = slice(b * per_column, (b + 1) * per_column)
        lanes = slice(b * tokens_here, (b + 1) * tokens_here)
        low_lanes = slice(latent + b * tokens_here, latent + (b + 1) * tokens_here)
        gathered[0, tokens_here : tokens_here + per_column, lanes] = table_high[rows, :]
        gathered[0, tokens_here : tokens_here + per_column, low_lanes] = table_low[rows, :]

    pl.semaphore_wait(barrier, 2 + (peers - 1) + (groups - 1))

    def gather_copy(way, step):
        target = on_ring(1 if way == 0 else -1)
        source = 0 if step == 0 else 2 * step - 1 + way
        if step < half - 1:
            src, dst = gathered.at[source], gathered.at[2 * step + 1 + way]
        else:
            lanes = pl.ds(way * latent, latent)
            src, dst = gathered.at[source, :, lanes], gathered.at[ring - 1, :, lanes]
        return pltpu.make_async_remote_copy(
            src_ref=src,
            dst_ref=dst,
            send_sem=gather_send.at[way, step],
            recv_sem=gather_recv.at[way, step],
            device_id=target,
            device_id_type=MESH,
        )

    earlier = (
        lax.broadcasted_iota(jnp.int32, (tokens_here, tokens_here), 0)
        < lax.broadcasted_iota(jnp.int32, (tokens_here, tokens_here), 1)
    ).astype(BF16)
    row_ids = lax.broadcasted_iota(jnp.int32, (per_column, tokens_here), 0)
    main_slots = lax.broadcasted_iota(jnp.int32, (MAIN, tokens_here), 0).astype(F32)

    def slot_copy(j, s, first, count):
        d = peer(j)
        rows = pl.ds(s * SET_ROWS + first, count)
        return pltpu.make_async_remote_copy(
            src_ref=send_rows.at[d, rows],
            dst_ref=expert_rows.at[place, rows],
            send_sem=slot_send.at[s, j],
            recv_sem=slot_recv.at[s, j],
            device_id=at_peer(d),
            device_id_type=MESH,
        )

    def own_slots(s, first, count):
        rows = pl.ds(s * SET_ROWS + first, count)
        return pltpu.make_async_copy(
            send_rows.at[place, rows], expert_rows.at[place, rows], own_sem.at[0, s]
        )

    def dispatch(i):
        s, within = i // SET, i % SET
        weights = []
        for b in range(columns):
            info = (
                gathered[i, tokens_here : tokens_here + per_column, b * tokens_here : (b + 1) * tokens_here].astype(F32)
                + gathered[
                    i,
                    tokens_here : tokens_here + per_column,
                    latent + b * tokens_here : latent + (b + 1) * tokens_here,
                ].astype(F32)
            )
            for c in range(CORES):
                weights.append(
                    jnp.sum(jnp.where(row_ids == z * CORES + c, info, 0.0), axis=0, keepdims=True)
                )
        weight = jnp.concatenate(weights, axis=0)
        named = weight > 0.0
        before = dot(named.astype(F32).astype(BF16), earlier)
        slot = jnp.where(named, before, -1.0)
        extra_rows = lax.broadcasted_iota(jnp.int32, (MAIN, tokens_here), 0)
        extra_slots = jnp.where(
            lax.div(extra_rows, EXTRA) == within, MAIN + lax.rem(extra_rows, EXTRA), -2
        ).astype(F32)
        hits = []
        for slots in (main_slots, extra_slots):
            for d in range(peers):
                hits.append((slots == slot[d : d + 1, :]).astype(F32))
        chosen = jnp.concatenate(hits, axis=0)
        weight_rows = jnp.concatenate(
            [jnp.broadcast_to(weight[d : d + 1, :], (MAIN, tokens_here)) for d in range(peers)], axis=0
        )
        weighted = chosen * jnp.concatenate([weight_rows, weight_rows], axis=0)
        pick[i] = chosen.astype(BF16)
        weigh[i] = weighted.astype(BF16)
        scale = jnp.sum(weighted, axis=1, keepdims=True)
        chosen = chosen.astype(BF16)
        main_count = peers * MAIN
        for part in range(2):
            lanes = slice(part * latent, (part + 1) * latent)
            rows = dot(chosen, gathered[i, 0:tokens_here, lanes])
            if part == 1:
                rows = rows * scale
            first = s * SET_ROWS + within * MAIN
            send_rows[:, first : first + MAIN, lanes] = (
                rows[:main_count].astype(BF16).reshape(peers, MAIN, latent)
            )
            extra = rows[main_count:]
            if within > 0:
                extra = extra + extra_sum[:, lanes]
            if within < SET - 1:
                extra_sum[:, lanes] = extra
            else:
                first = s * SET_ROWS + SET * MAIN
                send_rows[:, first : first + MAIN, lanes] = extra.astype(BF16).reshape(peers, MAIN, latent)
        count = MAIN if within < SET - 1 else 2 * MAIN

        def start(j, carry):
            slot_copy(j, s, within * MAIN, count).start()
            return carry

        lax.fori_loop(1, peers, start, 0)
        own_slots(s, within * MAIN, count).start()

    for way in range(2):
        gather_copy(way, 0).start()
    dispatch(0)
    for step in range(1, half):
        for way in range(2):
            gather_copy(way, step - 1).wait_recv()
            gather_copy(way, step).start()
        for way in range(2):
            dispatch(2 * step - 1 + way)
    for way in range(2):
        gather_copy(way, half - 1).wait_recv()
    dispatch(ring - 1)

    def back_copy(j, s):
        d = peer(j)
        rows = pl.ds(s * SET_ROWS, SET_ROWS)
        return pltpu.make_async_remote_copy(
            src_ref=result_rows.at[d, rows],
            dst_ref=back_rows.at[place, rows],
            send_sem=back_send.at[s, j],
            recv_sem=back_recv.at[s, j],
            device_id=at_peer(d),
            device_id_type=MESH,
        )

    def own_back(s):
        rows = pl.ds(s * SET_ROWS, SET_ROWS)
        return pltpu.make_async_copy(result_rows.at[place, rows], back_rows.at[place, rows], own_sem.at[1, s])

    tile = min(256, hidden)
    wide = min(256, latent)
    count = peers * SET_ROWS

    def expert(s):
        def arrived(j, carry):
            slot_copy(j, s, 0, SET_ROWS).wait_recv()
            return carry

        lax.fori_loop(1, peers, arrived, 0)
        own_slots(s, 0, SET_ROWS).wait()
        set_rows = slice(s * SET_ROWS, (s + 1) * SET_ROWS)

        def hidden_tile(h, carry):
            cols = pl.ds(pl.multiple_of(h * tile, tile), tile)
            rows_in = expert_rows[:, set_rows, 0:latent].reshape(count, latent)
            grad_in = expert_rows[:, set_rows, latent:].reshape(count, latent)
            pre_gate = dot(rows_in, gw_ref[:, cols])
            pre_up = dot(rows_in, uw_ref[:, cols])
            grad_act = dot(grad_in, ow_ref[cols, :], COLS)
            sig = 1.0 / (1.0 + jnp.exp(-pre_gate))
            swish = pre_gate * sig
            shape = (peers, SET_ROWS, tile)
            act[:, set_rows, cols] = (swish * pre_up).astype(BF16).reshape(shape)
            grad_gate[:, set_rows, cols] = (
                (grad_act * pre_up * (sig * (1.0 + pre_gate * (1.0 - sig)))).astype(BF16).reshape(shape)
            )
            grad_up[:, set_rows, cols] = (grad_act * swish).astype(BF16).reshape(shape)
            return carry

        lax.fori_loop(0, hidden // tile, hidden_tile, 0)

        def latent_tile(n, carry):
            cols = pl.ds(pl.multiple_of(n * wide, wide), wide)
            later = pl.ds(pl.multiple_of(latent + n * wide, wide), wide)
            shape = (peers, SET_ROWS, wide)
            out = dot(act[:, set_rows, :].reshape(count, hidden), ow_ref[:, cols])
            result_rows[:, set_rows, cols] = out.astype(BF16).reshape(shape)
            back = dot(grad_gate[:, set_rows, :].reshape(count, hidden), gw_ref[cols, :], COLS)
            back = back + dot(grad_up[:, set_rows, :].reshape(count, hidden), uw_ref[cols, :], COLS)
            result_rows[:, set_rows, later] = back.astype(BF16).reshape(shape)
            return carry

        lax.fori_loop(0, latent // wide, latent_tile, 0)

        def start(j, carry):
            back_copy(j, s).start()
            return carry

        lax.fori_loop(1, peers, start, 0)
        own_back(s).start()

    for s in range(sets):
        expert(s)

    share = hidden // groups
    all_rows = peers * sets * SET_ROWS

    def grad_copy(k):
        return pltpu.make_async_remote_copy(
            src_ref=grads_out.at[k],
            dst_ref=grads_in.at[k],
            send_sem=grad_send.at[k],
            recv_sem=grad_recv.at[k],
            device_id=group_at(k),
            device_id_type=MESH,
        )

    def weight_terms(k):
        cols = pl.ds(pl.multiple_of(lax.rem(my_group + k, groups) * share, share), share)
        rows_in = expert_rows[:, :, 0:latent].reshape(all_rows, latent)
        grad_in = expert_rows[:, :, latent:].reshape(all_rows, latent)
        gate_term = dot(rows_in, grad_gate[:, :, cols].reshape(all_rows, share), ROWS)
        up_term = dot(rows_in, grad_up[:, :, cols].reshape(all_rows, share), ROWS)
        out_term = dot(act[:, :, cols].reshape(all_rows, share), grad_in, ROWS)
        return gate_term, up_term, out_term

    def other_share(k, carry):
        gate_term, up_term, out_term = weight_terms(k)
        grads_out[k, 0:latent, 0:share] = gate_term.astype(BF16)
        grads_out[k, 0:latent, share:] = up_term.astype(BF16)
        grads_out[k, latent:, :] = out_term.astype(BF16)
        grad_copy(k).start()
        return carry

    lax.fori_loop(1, groups, other_share, 0)
    gate_grad_ref[...], up_grad_ref[...], out_grad_ref[...] = weight_terms(0)

    def combine(i):
        s, within = i // SET, i % SET
        first = s * SET_ROWS + within * MAIN
        extra = s * SET_ROWS + SET * MAIN
        shape = (peers * MAIN, latent)
        parts = []
        for part, matrix in enumerate((weigh, pick)):
            lanes = slice(part * latent, (part + 1) * latent)
            rows = jnp.concatenate(
                [
                    back_rows[:, first : first + MAIN, lanes].reshape(shape),
                    back_rows[:, extra : extra + MAIN, lanes].reshape(shape),
                ],
                axis=0,
            )
            parts.append(dot(matrix[i], rows, ROWS))
        return parts

    def ring_copy(way, step):
        lanes = pl.ds(way * latent, latent) if step == 0 else pl.ds(0, 2 * latent)
        return pltpu.make_async_remote_copy(
            src_ref=ring_out.at[way, step, :, lanes],
            dst_ref=ring_in.at[way, step, :, lanes],
            send_sem=ring_send.at[way, step],
            recv_sem=ring_recv.at[way, step],
            device_id=on_ring(-1 if way == 0 else 1),
            device_id_type=MESH,
        )

    def returned(s):
        def arrived(j, carry):
            back_copy(j, s).wait_recv()
            return carry

        lax.fori_loop(1, peers, arrived, 0)
        own_back(s).wait()

    waiting = set(range(sets))

    def ready(i):
        if i // SET in waiting:
            waiting.remove(i // SET)
            returned(i // SET)

    ready(ring - 1)
    parts = combine(ring - 1)
    for way in range(2):
        ring_out[way, 0, :, way * latent : (way + 1) * latent] = parts[way].astype(BF16)
        ring_copy(way, 0).start()
    for step in range(1, half):
        for way in range(2):
            i = 2 * (half - step) - 1 + way
            ready(i)
            parts = combine(i)
            ring_copy(way, step - 1).wait_recv()
            for part in range(2):
                lanes = slice(part * latent, (part + 1) * latent)
                value = parts[part]
                if step > 1 or part == way:
                    value = value + ring_in[way, step - 1, :, lanes].astype(F32)
                ring_out[way, step, :, lanes] = value.astype(BF16)
            ring_copy(way, step).start()
    ready(0)
    parts = combine(0)
    for way in range(2):
        ring_copy(way, half - 1).wait_recv()
    for part in range(2):
        lanes = slice(part * latent, (part + 1) * latent)
        value = parts[part]
        for way in range(2):
            if half > 1 or way == part:
                value = value + ring_in[way, half - 1, :, lanes].astype(F32)
        mid_ref[:, lanes] = value.astype(BF16)

    for k in range(1, groups):
        grad_copy(k).wait_recv()
        gate_grad_ref[...] += grads_in[k, 0:latent, 0:share].astype(F32)
        up_grad_ref[...] += grads_in[k, 0:latent, share:].astype(F32)
        out_grad_ref[...] += grads_in[k, latent:, :].astype(F32)

    for way in range(2):
        for step in range(half):
            gather_copy(way, step).wait_send()
            ring_copy(way, step).wait_send()

    def sent(j, carry):
        for s in range(sets):
            slot_copy(j, s, 0, SET_ROWS).wait_send()
            back_copy(j, s).wait_send()
        return carry

    lax.fori_loop(1, peers, sent, 0)
    for k in range(1, groups):
        grad_copy(k).wait_send()


def layer(ring, routes, gates, tokens, cotan, down, up, gate_weight, up_weight, out_weight):
    count, latent = tokens.shape[0], down.shape[1]
    hidden = gate_weight.shape[1]
    experts = lax.axis_size("expert")
    groups = lax.axis_size("dp")
    peers = experts // ring
    sets = ring // SET
    half = ring // 2
    share = hidden // groups
    chosen = 2 * peers * MAIN
    rows = sets * SET_ROWS
    vmem = pl.BlockSpec(memory_space=pltpu.VMEM)
    dma = pltpu.SemaphoreType.DMA
    return pl.pallas_call(
        partial(layer_kernel, ring),
        out_shape=(
            jax.ShapeDtypeStruct((count, 2 * latent), BF16),
            jax.ShapeDtypeStruct((latent, share), F32),
            jax.ShapeDtypeStruct((latent, share), F32),
            jax.ShapeDtypeStruct((share, latent), F32),
        ),
        in_specs=[vmem] * 9,
        out_specs=(vmem,) * 4,
        scratch_shapes=[
            pltpu.VMEM((ring, count + MAIN, 2 * latent), BF16),
            pltpu.VMEM((peers, rows, 2 * latent), BF16),
            pltpu.VMEM((peers, rows, 2 * latent), BF16),
            pltpu.VMEM((peers, rows, 2 * latent), BF16),
            pltpu.VMEM((peers, rows, 2 * latent), BF16),
            pltpu.VMEM((ring, chosen, count), BF16),
            pltpu.VMEM((ring, chosen, count), BF16),
            pltpu.VMEM((peers * MAIN, 2 * latent), F32),
            pltpu.VMEM((peers, rows, hidden), BF16),
            pltpu.VMEM((peers, rows, hidden), BF16),
            pltpu.VMEM((peers, rows, hidden), BF16),
            pltpu.VMEM((2, half, count, 2 * latent), BF16),
            pltpu.VMEM((2, half, count, 2 * latent), BF16),
            pltpu.VMEM((groups, latent + share, 2 * share), BF16),
            pltpu.VMEM((groups, latent + share, 2 * share), BF16),
            dma((2, half)),
            dma((2, half)),
            dma((sets, peers)),
            dma((sets, peers)),
            dma((sets, peers)),
            dma((sets, peers)),
            dma((2, sets)),
            dma((2, half)),
            dma((2, half)),
            dma((groups,)),
            dma((groups,)),
        ],
        compiler_params=pltpu.CompilerParams(
            collective_id=0, has_side_effects=True, vmem_limit_bytes=60 * 1024 * 1024
        ),
        name="layer",
    )(routes, gates, tokens, cotan, down, up, gate_weight, up_weight, out_weight)


def shards(
    ring,
    tokens,
    routes,
    gate_values,
    latent_down,
    gate_weight,
    up_weight,
    out_weight,
    latent_up,
    grad_mixed,
):
    latent = latent_down.shape[1]
    mid, gate_grad, up_grad, out_grad = layer(
        ring,
        routes.T,
        gate_values.T,
        tokens,
        grad_mixed,
        latent_down,
        latent_up,
        gate_weight[0],
        up_weight[0],
        out_weight[0],
    )
    combined, grad_latent = mid[:, :latent], mid[:, latent:]
    mixed = dot(combined, latent_up, COLS).astype(BF16)
    grad_tokens = dot(grad_latent, latent_down, COLS).astype(BF16)
    down_term = dot(tokens, grad_latent, ROWS).astype(BF16)
    up_term = dot(grad_mixed, combined, ROWS).astype(BF16)
    terms = jnp.concatenate([down_term, up_term], axis=1)
    terms = lax.psum_scatter(terms, "expert", scatter_dimension=0, tiled=True)
    terms = lax.psum(terms, "dp").astype(F32)
    return (
        mixed,
        grad_tokens,
        terms[:, :latent],
        terms[:, latent:],
        gate_grad[None],
        up_grad[None],
        out_grad[None],
    )


def solution(mesh, ring=RING):
    rows = P(("dp", "expert"), None)
    own = P("expert", None, None)
    return jax.shard_map(
        partial(shards, ring),
        mesh=mesh,
        in_specs=(rows, rows, rows, P(), own, own, own, P(), rows),
        out_specs=(
            rows,
            rows,
            P("expert", None),
            P("expert", None),
            P("expert", None, "dp"),
            P("expert", None, "dp"),
            P("expert", "dp", None),
        ),
        check_vma=False,
    )
```

time: 503 us -> 328 us (0.65)
  Pallas kernels: 0 us -> 109 us
  waiting for transfers between devices: 261 us -> 180 us
  local copies, waits for them, and re-layouts: 68.3 us -> 14.5 us
  blocking collectives: 52.7 us -> 0 us
  matrix products: 49.8 us -> 7.31 us
  other arithmetic: 35.9 us -> 2.56 us
  starting transfers between devices: 19.3 us -> 0.08 us
    pallas_call x0 -> x1, Pallas kernels: none -> 109 us  [layer(): pl.pallas_call(partial(layer_kernel, ring), out_shape=(jax.ShapeDtypeStru...]
    all_to_all x3 -> x0, waiting for transfers between devices: 78.9 us -> none  [the longest x1 28.4 us: shards(): lax.all_to_all(send_grad.reshape(send_shape), 'expert', split_axis=0, con...]
    all_to_all x1 -> x0, blocking collectives: 52.7 us -> none  [shards(): lax.all_to_all(send_latent.reshape(send_shape), 'expert', split_axis=0, c...]
    dot_general x15 -> x4, matrix products: 49.8 us -> 7.31 us  [dot(): return lax.dot_general(a, b, dims, preferred_element_type=F32)]
    gather x7 -> x0, local copies, waits for them, and re-layouts: 29 us -> none  [the longest x2 8.38 us: shards(): jnp.take(grad_comb, token_row, axis=0)]
    all_to_all x3 -> x0, starting transfers between devices: 18.9 us -> none  [the longest x1 6.3 us: shards(): lax.all_to_all(send_grad.reshape(send_shape), 'expert', split_axis=0, con...]
    another operation x3 -> x0, other arithmetic: 18.2 us -> none
    reshape x7 -> x0, local copies, waits for them, and re-layouts: 16.6 us -> none  [the longest x2 4.58 us: flatten_rows(): return values.reshape(-1, values.shape[-1])]
  transfers between devices with their start and end apart: 8 -> 2, of which waited for: 5 -> 2; matrix products, arithmetic and copies ran while one was open for 15% -> 1% of each run, Pallas kernels for 0% -> 0%
where the time goes in v1:
time: 328 us; the launch traced here: 327 us
  waiting for transfers between devices  180 us (55%)
  Pallas kernels  109 us (33%)
  local copies, waits for them, and re-layouts  14.5 us (4%)
  between operations  14.1 us (4%)
  matrix products  7.31 us (2%)
    unnamed x3, waiting for transfers between devices  134 us
    pallas_call x1, Pallas kernels, layer(): pl.pallas_call(partial(layer_kernel, ring), out_shape=(jax.ShapeDtypeStru...  109 us
    psum x1, waiting for transfers between devices, shards(): terms = lax.psum(terms, 'dp').astype(F32)  46.1 us
    unnamed x21, local copies, waits for them, and re-layouts  13.5 us
    dot_general x4, matrix products, dot(): return lax.dot_general(a, b, dims, preferred_element_type=F32)  7.31 us
  transfers between devices with their start and end apart: 2, of which 2 were waited for; matrix products, arithmetic and copies ran while one was open for 1% of the time, Pallas kernels for 0%

profile of v1, /device:TPU:1, one launch (start us, length us, event | category | flops | bytes accessed | tf_op | source)
XLA Modules:
  0.0 326.9 jit_solution(14763298853101664366)
XLA Ops:
  7.2 0.0 reduce-scatter.4.cloned.1.call-start
  7.2 0.0 copy-start.1
  7.2 108.5 %layer.1 = (bf16[128,1024]{1,0:T(8,128)(2,1)}, f32[512,256]{1,0:T(8,128)}, f32[512,256]{1,0:T(8,128)}, f32[256,512]{1,0:T(8,128)}) custom-call(s32[8,128]{1,0:T(8,128)} %bitcast.23, f32[8,128]{1,0:T(8,128)} %bitcast.24, bf16[128,2048]{1,0:T(8,128)(2,1)} %tokens_ref.1, bf16[128,2048]{1,0:T(8,128)(2,1)} %cotan_ref.1, bf16[2048,512]{1,0:T(8,128)(2,1)} %down_ref.1, ...), custom_call_target="tpu_custom_call" | custom-call | tf_op jit(solution)/shard_map/layer/pallas_call | solution.py:457
  115.7 0.0 copy-start.2
  115.8 0.0 copy-start.3
  115.8 0.0 copy-done.1
  115.8 1.7 fusion
  117.5 0.0 copy-done.2
  117.5 0.0 copy-done.3
  117.5 0.7 fusion.1
  118.2 2.6 pad_maximum_fusion
  120.8 6.4 %copy.20 = bf16[2048,1024]{1,0:T(8,128)(2,1)} copy(bf16[2048,1024]{0,1:T(8,128)(2,1)} %pad_maximum_fusion) | data formatting | bytes 8388608
  127.2 0.0 reduce-scatter.4.cloned.1.call-update
  127.2 0.0 all-reduce.2.cloned.1.call-start
  127.3 1.5 copy-done
  128.8 1.6 convolution_convert_fusion.2
  130.4 133.7 %reduce-scatter.4.cloned.1.call-done = bf16[32,1024]{1,0:T(8,128)(2,1)} async-done(((bf16[2048,1024]{1,0:T(8,128)(2,1)}), bf16[32,1024]{1,0:T(8,128)(2,1)}) %reduce-scatter.4.cloned.1.call-update) | async-done | bytes 65552
  264.1 1.7 copy.21
  265.7 0.0 all-reduce.2.cloned.1.call-update
  265.8 0.0 copy-start.6
  265.8 0.0 copy-start.5
  265.8 3.3 %convolution_convert_fusion.3 = bf16[128,2048]{1,0:T(8,128)(2,1)} fusion(bf16[2048,512]{1,0:T(8,128)(2,1)} %up_ref.1, bf16[128,1024]{1,0:T(8,128)(2,1)S(1)} %copy-done.3), kind=kOutput, calls=%fused_computation.6 | convolution fusion | flops 268697600 | bytes 2752512 | tf_op jit(solution)/shard_map/dot_general | solution.py:27
  269.1 46.1 %all-reduce.2.cloned.1.call-done = bf16[32,1024]{0,1:T(8,128)(2,1)} async-done(((bf16[32,1024]{0,1:T(8,128)(2,1)}), bf16[32,1024]{0,1:T(8,128)(2,1)}) %all-reduce.2.cloned.1.call-update) | async-done | bytes 65552 | tf_op jit(solution)/shard_map/psum | solution.py:534
  315.2 1.0 fusion.6
  316.2 0.7 copy.18
  316.9 0.7 copy.19
  317.7 0.0 copy-done.6
  317.7 0.8 copy.26
  318.4 0.0 copy-done.5
  318.4 0.8 copy.27
  319.2 0.0 copy-done.4
  319.2 0.8 copy.28
  (2 shorter events, 0.0 us)
Async XLA Ops:
  7.2 256.9 %reduce-scatter.4.cloned.1.call-start = ((), (), s32[]{:S(2)}) async-start(), calls=%async_computation.2 | async-start | bytes 4259840
  7.2 108.6 %copy-start.1 = (bf16[128,2048]{1,0:T(8,128)(2,1)S(1)}, bf16[128,2048]{1,0:T(8,128)(2,1)}, u32[]{:S(2)}) copy-start(bf16[128,2048]{1,0:T(8,128)(2,1)} %tokens_ref.1) | copy-start | bytes 1572868
  115.7 1.7 copy-start.2
  115.8 1.7 copy-start.3
  127.2 1.6 copy-start
  127.2 187.9 %all-reduce.2.cloned.1.call-start = ((), (), s32[]{:S(2)}) async-start(), calls=%async_computation.1 | async-start | bytes 524288 | tf_op jit(solution)/shard_map/psum | solution.py:534
  265.8 51.9 %copy-start.6 = (f32[512,256]{1,0:T(8,128)S(1)}, f32[512,256]{1,0:T(8,128)}, u32[]{:S(2)}) copy-start(f32[512,256]{1,0:T(8,128)} %get-tuple-element.12) | copy-start | bytes 1572868
  265.8 52.7 %copy-start.5 = (f32[512,256]{1,0:T(8,128)S(1)}, f32[512,256]{1,0:T(8,128)}, u32[]{:S(2)}) copy-start(f32[512,256]{1,0:T(8,128)} %get-tuple-element.13) | copy-start | bytes 1572868
  269.1 50.2 %copy-start.4 = (f32[256,512]{1,0:T(8,128)S(1)}, f32[256,512]{1,0:T(8,128)}, u32[]{:S(2)}) copy-start(f32[256,512]{1,0:T(8,128)} %get-tuple-element.14) | copy-start | bytes 1572868
Sparse Core Ops, SparseCore 0:
  127.3 136.6 reduce-scatter.3
  267.1 48.0 all-reduce.1

commit v2 on v1

--- a/solution.py
+++ b/solution.py
@@ -38,10 +38,23 @@
     gw_ref,
     uw_ref,
     ow_ref,
-    mid_ref,
+    mixed_ref,
+    token_grad_ref,
+    down_grad_ref,
+    up_proj_grad_ref,
     gate_grad_ref,
     up_grad_ref,
     out_grad_ref,
+    mid,
+    sides,
+    lates,
+    x_out,
+    x_in,
+    x_sum,
+    z_out,
+    z_in,
+    last_out,
+    last_in,
     gathered,
     send_rows,
     expert_rows,
@@ -68,6 +81,17 @@
     ring_recv,
     grad_send,
     grad_recv,
+    side_send,
+    side_recv,
+    relay_send,
+    late_send,
+    late_recv,
+    x_send,
+    x_recv,
+    z_send,
+    z_recv,
+    last_send,
+    last_recv,
 ):
     tokens_here, latent = tokens_ref.shape[0], down_ref.shape[1]
     hidden = gw_ref.shape[1]
@@ -96,13 +120,18 @@
     def group_at(k):
         return (lax.rem(my_group + k, groups), me)
 
+    def mate(k, c):
+        return (lax.rem(my_group + k, groups), me - core + c)
+
+    mates = [(k, c) for k in range(1, groups) for c in range(CORES)] + [(0, 1 - core)]
+
     barrier = pltpu.get_barrier_semaphore()
-    for step in (1, -1):
+    for step in range(1, ring):
         pl.semaphore_signal(barrier, inc=1, device_id=on_ring(step), device_id_type=MESH)
     for j in range(1, peers):
         pl.semaphore_signal(barrier, inc=1, device_id=at_peer(peer(j)), device_id_type=MESH)
-    for k in range(1, groups):
-        pl.semaphore_signal(barrier, inc=1, device_id=group_at(k), device_id_type=MESH)
+    for k, c in mates:
+        pl.semaphore_signal(barrier, inc=1, device_id=mate(k, c), device_id_type=MESH)
 
     gathered[0, 0:tokens_here, 0:latent] = dot(tokens_ref[...], down_ref[...]).astype(BF16)
     gathered[0, 0:tokens_here, latent:] = dot(cotan_ref[...], up_ref[...]).astype(BF16)
@@ -120,7 +149,7 @@
         gathered[0, tokens_here : tokens_here + per_column, lanes] = table_high[rows, :]
         gathered[0, tokens_here : tokens_here + per_column, low_lanes] = table_low[rows, :]
 
-    pl.semaphore_wait(barrier, 2 + (peers - 1) + (groups - 1))
+    pl.semaphore_wait(barrier, (ring - 1) + (peers - 1) + len(mates))
 
     def gather_copy(way, step):
         target = on_ring(1 if way == 0 else -1)
@@ -228,9 +257,56 @@
         lax.fori_loop(1, peers, start, 0)
         own_slots(s, within * MAIN, count).start()
 
+    def side_copy(k, c, source):
+        return pltpu.make_async_remote_copy(
+            src_ref=source,
+            dst_ref=sides.at[k, core],
+            send_sem=side_send.at[k, c],
+            recv_sem=side_recv.at[k, core],
+            device_id=mate(k, c),
+            device_id_type=MESH,
+        )
+
+    def side_arrived(k, c):
+        pltpu.make_async_remote_copy(
+            src_ref=tokens_ref,
+            dst_ref=sides.at[k, c],
+            send_sem=side_send.at[k, c],
+            recv_sem=side_recv.at[k, c],
+            device_id=mate(k, c),
+            device_id_type=MESH,
+        ).wait_recv()
+
+    across = groups // 2
+
+    def relay_copy(c):
+        step = 1 - 2 * core
+        return pltpu.make_async_remote_copy(
+            src_ref=sides.at[1 + (groups - 2) * core, c],
+            dst_ref=sides.at[across, c],
+            send_sem=relay_send.at[c],
+            recv_sem=side_recv.at[across, c],
+            device_id=(lax.rem(my_group + step + groups, groups), me),
+            device_id_type=MESH,
+        )
+
     for way in range(2):
         gather_copy(way, 0).start()
     dispatch(0)
+    near = sorted({1, groups - 1})
+    for k in near:
+        for c, source in enumerate((tokens_ref, cotan_ref)):
+            side_copy(k, c, source).start()
+
+    @pl.when(core == 0)
+    def _():
+        side_copy(0, 1, cotan_ref).start()
+
+    @pl.when(core == 1)
+    def _():
+        side_copy(0, 0, tokens_ref).start()
+
+    sides[0, core] = jnp.where(core == 0, tokens_ref[...], cotan_ref[...])
     for step in range(1, half):
         for way in range(2):
             gather_copy(way, step - 1).wait_recv()
@@ -308,6 +384,13 @@
 
         lax.fori_loop(1, peers, start, 0)
         own_back(s).start()
+
+    for c in range(CORES):
+        for k in near:
+            side_arrived(k, c)
+    if across > 1:
+        for c in range(CORES):
+            relay_copy(c).start()
 
     for s in range(sets):
         expert(s)
@@ -417,13 +500,136 @@
         for way in range(2):
             if half > 1 or way == part:
                 value = value + ring_in[way, half - 1, :, lanes].astype(F32)
-        mid_ref[:, lanes] = value.astype(BF16)
+        mid[:, lanes] = value.astype(BF16)
+
+    block = latent // groups
+    features = tokens_ref.shape[1]
+    column_rows = features // columns
+    ring_rows = column_rows // ring
+    last_rows = ring_rows // CORES
+
+    def late_lanes(k, c):
+        start = latent * (1 - c) + block * lax.rem(my_group + k, groups)
+        return pl.ds(pl.multiple_of(start, block), block)
+
+    def late_copy(k, c):
+        return pltpu.make_async_remote_copy(
+            src_ref=mid.at[:, late_lanes(k, c)],
+            dst_ref=lates.at[k, core],
+            send_sem=late_send.at[k, c],
+            recv_sem=late_recv.at[k, core],
+            device_id=mate(k, c),
+            device_id_type=MESH,
+        )
+
+    def late_arrived(k, c):
+        pltpu.make_async_remote_copy(
+            src_ref=lates.at[k, c],
+            dst_ref=lates.at[k, c],
+            send_sem=late_send.at[k, c],
+            recv_sem=late_recv.at[k, c],
+            device_id=mate(k, c),
+            device_id_type=MESH,
+        ).wait_recv()
+
+    for k, c in mates:
+        late_copy(k, c).start()
+    lates[0, core] = mid[:, late_lanes(0, core)]
+    mixed_ref[...] = dot(mid[:, 0:latent], up_ref[...], COLS).astype(BF16)
+    token_grad_ref[...] = dot(mid[:, latent:], down_ref[...], COLS).astype(BF16)
+
+    side_arrived(0, 1 - core)
+    if across > 1:
+        for c in range(CORES):
+            side_arrived(across, c)
+    for k, c in mates:
+        late_arrived(k, c)
+    both = groups * CORES * tokens_here
+
+    def term_rows(k):
+        cols = pl.ds(pl.multiple_of(lax.rem(lax.div(me, ring * CORES) + k, columns) * column_rows, column_rows), column_rows)
+        term = dot(lates[...].reshape(both, block), sides[:, :, :, cols].reshape(both, column_rows), ROWS)
+        return term.T
+
+    def x_copy(k):
+        return pltpu.make_async_remote_copy(
+            src_ref=x_out.at[k],
+            dst_ref=x_in.at[k],
+            send_sem=x_send.at[k],
+            recv_sem=x_recv.at[k],
+            device_id=at_peer(peer(k * CORES)),
+            device_id_type=MESH,
+        )
+
+    for k in range(1, columns):
+        x_out[k] = term_rows(k).astype(BF16)
+        x_copy(k).start()
+    total = term_rows(0)
+    for k in range(1, columns):
+        x_copy(k).wait_recv()
+        total = total + x_in[k].astype(F32)
+    x_sum[...] = total.reshape(ring, ring_rows, block)
+    z_out[...] = x_sum[...].astype(BF16)
+
+    def z_copy(r):
+        return pltpu.make_async_remote_copy(
+            src_ref=z_out.at[lax.rem(z + r, ring)],
+            dst_ref=z_in.at[r],
+            send_sem=z_send.at[r],
+            recv_sem=z_recv.at[r],
+            device_id=on_ring(r),
+            device_id_type=MESH,
+        )
+
+    for r in range(1, ring):
+        z_copy(r).start()
+    total = x_sum[z]
+    for r in range(1, ring):
+        z_copy(r).wait_recv()
+        total = total + z_in[r].astype(F32)
+    last_out[...] = total.reshape(CORES, last_rows, block)
+
+    def last_copy(k, c, slot):
+        return pltpu.make_async_remote_copy(
+            src_ref=last_out.at[c],
+            dst_ref=last_in.at[k, slot],
+            send_sem=last_send.at[k, c],
+            recv_sem=last_recv.at[k, slot],
+            device_id=mate(k, c),
+            device_id_type=MESH,
+        )
+
+    for k, c in mates:
+        last_copy(k, c, core).start()
+    last_in[0, core] = last_out[core]
 
     for k in range(1, groups):
         grad_copy(k).wait_recv()
         gate_grad_ref[...] += grads_in[k, 0:latent, 0:share].astype(F32)
         up_grad_ref[...] += grads_in[k, 0:latent, share:].astype(F32)
         out_grad_ref[...] += grads_in[k, latent:, :].astype(F32)
+
+    for k, c in mates:
+        last_copy(k, c, c).wait_recv()
+    for k in range(groups):
+        lanes = pl.ds(pl.multiple_of(lax.rem(my_group + groups - k, groups) * block, block), block)
+        down_grad_ref[:, lanes] = last_in[k, 0]
+        up_proj_grad_ref[:, lanes] = last_in[k, 1]
+
+    for k in near:
+        for c in range(CORES):
+            side_copy(k, c, tokens_ref).wait_send()
+    side_copy(0, 1 - core, tokens_ref).wait_send()
+    if across > 1:
+        for c in range(CORES):
+            relay_copy(c).wait_send()
+    for k, c in mates:
+        late_copy(k, c).wait_send()
+        last_copy(k, c, core).wait_send()
+    for k in range(1, columns):
+        x_copy(k).wait_send()
+    for r in range(1, ring):
+        z_copy(r).wait_send()
 
     for way in range(2):
         for step in range(half):
@@ -452,19 +658,37 @@
     share = hidden // groups
     chosen = 2 * peers * MAIN
     rows = sets * SET_ROWS
+    features = tokens.shape[1]
+    columns = peers // CORES
+    block = latent // groups
+    last_rows = features // experts
+    ring_rows = last_rows * CORES
     vmem = pl.BlockSpec(memory_space=pltpu.VMEM)
     dma = pltpu.SemaphoreType.DMA
     return pl.pallas_call(
         partial(layer_kernel, ring),
         out_shape=(
-            jax.ShapeDtypeStruct((count, 2 * latent), BF16),
+            jax.ShapeDtypeStruct((count, features), BF16),
+            jax.ShapeDtypeStruct((count, features), BF16),
+            jax.ShapeDtypeStruct((last_rows, latent), F32),
+            jax.ShapeDtypeStruct((last_rows, latent), F32),
             jax.ShapeDtypeStruct((latent, share), F32),
             jax.ShapeDtypeStruct((latent, share), F32),
             jax.ShapeDtypeStruct((share, latent), F32),
         ),
         in_specs=[vmem] * 9,
-        out_specs=(vmem,) * 4,
+        out_specs=(vmem,) * 7,
         scratch_shapes=[
+            pltpu.VMEM((count, 2 * latent), BF16),
+            pltpu.VMEM((groups, CORES, count, features), BF16),
+            pltpu.VMEM((groups, CORES, count, block), BF16),
+            pltpu.VMEM((columns, features // columns, block), BF16),
+            pltpu.VMEM((columns, features // columns, block), BF16),
+            pltpu.VMEM((ring, ring_rows, block), F32),
+            pltpu.VMEM((ring, ring_rows, block), BF16),
+            pltpu.VMEM((ring, ring_rows, block), BF16),
+            pltpu.VMEM((CORES, last_rows, block), F32),
+            pltpu.VMEM((groups, CORES, last_rows, block), F32),
             pltpu.VMEM((ring, count + MAIN, 2 * latent), BF16),
             pltpu.VMEM((peers, rows, 2 * latent), BF16),
             pltpu.VMEM((peers, rows, 2 * latent), BF16),
@@ -491,6 +715,17 @@
             dma((2, half)),
             dma((groups,)),
             dma((groups,)),
+            dma((groups, CORES)),
+            dma((groups, CORES)),
+            dma((CORES,)),
+            dma((groups, CORES)),
+            dma((groups, CORES)),
+            dma((columns,)),
+            dma((columns,)),
+            dma((ring,)),
+            dma((ring,)),
+            dma((groups, CORES)),
+            dma((groups, CORES)),
         ],
         compiler_params=pltpu.CompilerParams(
             collective_id=0, has_side_effects=True, vmem_limit_bytes=60 * 1024 * 1024
@@ -511,8 +746,7 @@
     latent_up,
     grad_mixed,
 ):
-    latent = latent_down.shape[1]
-    mid, gate_grad, up_grad, out_grad = layer(
+    mixed, grad_tokens, down_grad, up_proj_grad, gate_grad, up_grad, out_grad = layer(
         ring,
         routes.T,
         gate_values.T,
@@ -524,23 +758,7 @@
         up_weight[0],
         out_weight[0],
     )
-    combined, grad_latent = mid[:, :latent], mid[:, latent:]
-    mixed = dot(combined, latent_up, COLS).astype(BF16)
-    grad_tokens = dot(grad_latent, latent_down, COLS).astype(BF16)
-    down_term = dot(tokens, grad_latent, ROWS).astype(BF16)
-    up_term = dot(grad_mixed, combined, ROWS).astype(BF16)
-    terms = jnp.concatenate([down_term, up_term], axis=1)
-    terms = lax.psum_scatter(terms, "expert", scatter_dimension=0, tiled=True)
-    terms = lax.psum(terms, "dp").astype(F32)
-    return (
-        mixed,
-        grad_tokens,
-        terms[:, :latent],
-        terms[:, latent:],
-        gate_grad[None],
-        up_grad[None],
-        out_grad[None],
-    )
+    return mixed, grad_tokens, down_grad, up_proj_grad, gate_grad[None], up_grad[None], out_grad[None]
 
 
 def solution(mesh, ring=RING):

time: 328 us -> 142 us (0.43)
  waiting for transfers between devices: 180 us -> 0 us
  Pallas kernels: 109 us -> 134 us
  between operations: 14.1 us -> 0.69 us
  matrix products: 7.31 us -> 0 us
  local copies, waits for them, and re-layouts: 14.5 us -> 7.54 us
    unnamed x3 -> x0, waiting for transfers between devices: 134 us -> none
    psum x1 -> x0, waiting for transfers between devices: 46.1 us -> none  [shards(): terms = lax.psum(terms, 'dp').astype(F32)]
    pallas_call x1, Pallas kernels: 109 us -> 134 us  [layer(): pl.pallas_call(partial(layer_kernel, ring), out_shape=(jax.ShapeDtypeStru...]
    dot_general x4 -> x0, matrix products: 7.31 us -> none  [dot(): return lax.dot_general(a, b, dims, preferred_element_type=F32)]
    unnamed x21 -> x17, local copies, waits for them, and re-layouts: 13.5 us -> 7.54 us
  transfers between devices with their start and end apart: 2 -> 0, of which waited for: 2 -> 0; matrix products, arithmetic and copies ran while one was open for 1% -> 0% of each run, Pallas kernels for 0% -> 0%
where the time goes in v2:
time: 142 us
  Pallas kernels  134 us (94%)
  local copies, waits for them, and re-layouts  7.54 us (5%)
    pallas_call x1, Pallas kernels, layer(): pl.pallas_call(partial(layer_kernel, ring), out_shape=(jax.ShapeDtypeStru...  134 us
    unnamed x17, local copies, waits for them, and re-layouts  7.54 us

profile of v2, /device:TPU:1, one launch (start us, length us, event | category | flops | bytes accessed | tf_op | source)
XLA Modules:
  0.0 141.9 jit_solution(3527509509192724603)
XLA Ops:
  0.6 133.7 %layer.1 = (bf16[128,2048]{1,0:T(8,128)(2,1)}, bf16[128,2048]{1,0:T(8,128)(2,1)}, f32[32,512]{1,0:T(8,128)}, f32[32,512]{1,0:T(8,128)}, f32[512,256]{1,0:T(8,128...) custom-call(s32[8,128]{1,0:T(8,128)} %bitcast.14, f32[8,128]{1,0:T(8,128)} %bitcast.15, bf16[128,2048]{1,0:T(8,128)(2,1)} %tokens_ref.1, ...), custom_call_target="tpu_custom_call" | custom-call | tf_op jit(solution)/shard_map/layer/pallas_call | solution.py:668
  134.4 0.0 copy-start.4
  134.4 0.0 copy-start.3
  134.4 0.0 copy-start.2
  134.4 0.0 copy-start.1
  134.4 0.0 copy-start
  134.4 2.0 %copy.23 = bf16[128,2048]{1,0:T(8,128)(2,1)} copy(bf16[128,2048]{1,0:T(8,128)(2,1)} %get-tuple-element.28) | data formatting | bytes 1048576
  136.4 1.9 %copy.24 = bf16[128,2048]{1,0:T(8,128)(2,1)} copy(bf16[128,2048]{1,0:T(8,128)(2,1)} %get-tuple-element.29) | data formatting | bytes 1048576
  138.3 0.0 copy-done.4
  138.3 0.6 copy.25
  138.9 0.0 copy-done.3
  138.9 0.6 copy.26
  139.6 0.0 copy-done.2
  139.6 0.8 copy.27
  140.3 0.0 copy-done.1
  140.4 0.8 copy.28
  141.1 0.0 copy-done
  141.1 0.8 copy.29
Async XLA Ops:
  134.4 3.9 %copy-start.4 = (f32[32,512]{1,0:T(8,128)S(1)}, f32[32,512]{1,0:T(8,128)}, u32[]{:S(2)}) copy-start(f32[32,512]{1,0:T(8,128)} %get-tuple-element.30) | copy-start | bytes 196612
  134.4 4.6 %copy-start.3 = (f32[32,512]{1,0:T(8,128)S(1)}, f32[32,512]{1,0:T(8,128)}, u32[]{:S(2)}) copy-start(f32[32,512]{1,0:T(8,128)} %get-tuple-element.31) | copy-start | bytes 196612
  134.4 5.2 %copy-start.2 = (f32[512,256]{1,0:T(8,128)S(1)}, f32[512,256]{1,0:T(8,128)}, u32[]{:S(2)}) copy-start(f32[512,256]{1,0:T(8,128)} %get-tuple-element.18) | copy-start | bytes 1572868
  134.4 6.0 %copy-start.1 = (f32[512,256]{1,0:T(8,128)S(1)}, f32[512,256]{1,0:T(8,128)}, u32[]{:S(2)}) copy-start(f32[512,256]{1,0:T(8,128)} %get-tuple-element.19) | copy-start | bytes 1572868
  134.4 6.8 %copy-start = (f32[256,512]{1,0:T(8,128)S(1)}, f32[256,512]{1,0:T(8,128)}, u32[]{:S(2)}) copy-start(f32[256,512]{1,0:T(8,128)} %get-tuple-element.20) | copy-start | bytes 1572868

commit v3 on v2

--- a/solution.py
+++ b/solution.py
@@ -31,6 +31,20 @@
     ring,
     routes_ref,
     gates_ref,
+    tokens_hbm,
+    cotan_hbm,
+    down_hbm,
+    up_hbm,
+    gw_hbm,
+    uw_hbm,
+    ow_hbm,
+    mixed_hbm,
+    token_grad_hbm,
+    down_grad_hbm,
+    up_proj_grad_hbm,
+    gate_grad_hbm,
+    up_grad_hbm,
+    out_grad_hbm,
     tokens_ref,
     cotan_ref,
     down_ref,
@@ -45,6 +59,8 @@
     gate_grad_ref,
     up_grad_ref,
     out_grad_ref,
+    load_sem,
+    store_sem,
     mid,
     sides,
     lates,
@@ -133,40 +149,78 @@
     for k, c in mates:
         pl.semaphore_signal(barrier, inc=1, device_id=mate(k, c), device_id_type=MESH)
 
-    gathered[0, 0:tokens_here, 0:latent] = dot(tokens_ref[...], down_ref[...]).astype(BF16)
-    gathered[0, 0:tokens_here, latent:] = dot(cotan_ref[...], up_ref[...]).astype(BF16)
+    loads = [
+        pltpu.make_async_copy(src, dst, load_sem.at[n])
+        for n, (src, dst) in enumerate(
+            (
+                (tokens_hbm, tokens_ref),
+                (down_hbm, down_ref),
+                (cotan_hbm, cotan_ref),
+                (up_hbm, up_ref),
+                (gw_hbm, gw_ref),
+                (uw_hbm, uw_ref),
+                (ow_hbm, ow_ref),
+            )
+        )
+    ]
+    stores = [
+        pltpu.make_async_copy(src, dst, store_sem.at[n])
+        for n, (src, dst) in enumerate(
+            (
+                (mixed_ref, mixed_hbm),
+                (token_grad_ref, token_grad_hbm),
+                (down_grad_ref, down_grad_hbm),
+                (up_proj_grad_ref, up_proj_grad_hbm),
+                (gate_grad_ref, gate_grad_hbm),
+                (up_grad_ref, up_grad_hbm),
+                (out_grad_ref, out_grad_hbm),
+            )
+        )
+    ]
+    for load in loads[:4]:
+        load.start()
+
     expert_ids = lax.broadcasted_iota(jnp.int32, (experts, tokens_here), 0)
     table = jnp.zeros((experts, tokens_here), F32)
     for k in range(routes_ref.shape[0]):
         table = table + jnp.where(expert_ids == routes_ref[k : k + 1, :], gates_ref[k : k + 1, :], 0.0)
-    table_high = table.astype(BF16)
-    table_low = (table - table_high.astype(F32)).astype(BF16)
+    table = table.astype(BF16)
     per_column = ring * CORES
     for b in range(columns):
         rows = slice(b * per_column, (b + 1) * per_column)
         lanes = slice(b * tokens_here, (b + 1) * tokens_here)
-        low_lanes = slice(latent + b * tokens_here, latent + (b + 1) * tokens_here)
-        gathered[0, tokens_here : tokens_here + per_column, lanes] = table_high[rows, :]
-        gathered[0, tokens_here : tokens_here + per_column, low_lanes] = table_low[rows, :]
-
+        gathered[0, tokens_here : tokens_here + per_column, lanes] = table[rows, :]
+
+    def gather_copy(way, step, part):
+        source = 0 if step == 0 else 2 * step - 1 + way
+        target = 2 * step + 1 + way if step < half - 1 else ring - 1
+        rows = pl.ds(0, tokens_here + MAIN if part == 0 else tokens_here)
+        lanes = pl.ds(part * latent, latent)
+        return pltpu.make_async_remote_copy(
+            src_ref=gathered.at[source, rows, lanes],
+            dst_ref=gathered.at[target, rows, lanes],
+            send_sem=gather_send.at[way, step, part],
+            recv_sem=gather_recv.at[way, step, part],
+            device_id=on_ring(1 if way == 0 else -1),
+            device_id_type=MESH,
+        )
+
+    def gather_pieces(step):
+        return [(way, part) for part in range(2) for way in range(2) if step < half - 1 or part == way]
+
+    loads[0].wait()
+    loads[1].wait()
+    gathered[0, 0:tokens_here, 0:latent] = dot(tokens_ref[...], down_ref[...]).astype(BF16)
     pl.semaphore_wait(barrier, (ring - 1) + (peers - 1) + len(mates))
-
-    def gather_copy(way, step):
-        target = on_ring(1 if way == 0 else -1)
-        source = 0 if step == 0 else 2 * step - 1 + way
-        if step < half - 1:
-            src, dst = gathered.at[source], gathered.at[2 * step + 1 + way]
-        else:
-            lanes = pl.ds(way * latent, latent)
-            src, dst = gathered.at[source, :, lanes], gathered.at[ring - 1, :, lanes]
-        return pltpu.make_async_remote_copy(
-            src_ref=src,
-            dst_ref=dst,
-            send_sem=gather_send.at[way, step],
-            recv_sem=gather_recv.at[way, step],
-            device_id=target,
-            device_id_type=MESH,
-        )
+    for way in range(2):
+        gather_copy(way, 0, 0).start()
+    loads[2].wait()
+    loads[3].wait()
+    gathered[0, 0:tokens_here, latent:] = dot(cotan_ref[...], up_ref[...]).astype(BF16)
+    for way in range(2):
+        gather_copy(way, 0, 1).start()
+    for load in loads[4:]:
+        load.start()
 
     earlier = (
         lax.broadcasted_iota(jnp.int32, (tokens_here, tokens_here), 0)
@@ -175,87 +229,84 @@
     row_ids = lax.broadcasted_iota(jnp.int32, (per_column, tokens_here), 0)
     main_slots = lax.broadcasted_iota(jnp.int32, (MAIN, tokens_here), 0).astype(F32)
 
-    def slot_copy(j, s, first, count):
+    def slot_copy(j, s, first, count, lanes):
         d = peer(j)
         rows = pl.ds(s * SET_ROWS + first, count)
         return pltpu.make_async_remote_copy(
-            src_ref=send_rows.at[d, rows],
-            dst_ref=expert_rows.at[place, rows],
+            src_ref=send_rows.at[d, rows, lanes],
+            dst_ref=expert_rows.at[place, rows, lanes],
             send_sem=slot_send.at[s, j],
             recv_sem=slot_recv.at[s, j],
             device_id=at_peer(d),
             device_id_type=MESH,
         )
 
-    def own_slots(s, first, count):
+    def own_slots(s, first, count, lanes):
         rows = pl.ds(s * SET_ROWS + first, count)
         return pltpu.make_async_copy(
-            send_rows.at[place, rows], expert_rows.at[place, rows], own_sem.at[0, s]
-        )
-
-    def dispatch(i):
+            send_rows.at[place, rows, lanes], expert_rows.at[place, rows, lanes], own_sem.at[0, s]
+        )
+
+    all_lanes = pl.ds(0, 2 * latent)
+
+    def table_rows(i):
+        found = []
+        for b in range(columns):
+            first = b * tokens_here
+            info = gathered[i, tokens_here : tokens_here + per_column, first : first + tokens_here].astype(F32)
+            for c in range(CORES):
+                found.append(jnp.sum(jnp.where(row_ids == z * CORES + c, info, 0.0), axis=0, keepdims=True))
+        return jnp.concatenate(found, axis=0)
+
+    main_count = peers * MAIN
+
+    def dispatch(i, part):
         s, within = i // SET, i % SET
-        weights = []
-        for b in range(columns):
-            info = (
-                gathered[i, tokens_here : tokens_here + per_column, b * tokens_here : (b + 1) * tokens_here].astype(F32)
-                + gathered[
-                    i,
-                    tokens_here : tokens_here + per_column,
-                    latent + b * tokens_here : latent + (b + 1) * tokens_here,
-                ].astype(F32)
+        lanes = slice(part * latent, (part + 1) * latent)
+        if part == 0:
+            named = table_rows(i) > 0.0
+            before = dot(named.astype(F32).astype(BF16), earlier)
+            slot = jnp.where(named, before, -1.0)
+            extra_rows = lax.broadcasted_iota(jnp.int32, (MAIN, tokens_here), 0)
+            extra_slots = jnp.where(
+                lax.div(extra_rows, EXTRA) == within, MAIN + lax.rem(extra_rows, EXTRA), -2
+            ).astype(F32)
+            hits = []
+            for slots in (main_slots, extra_slots):
+                for d in range(peers):
+                    hits.append((slots == slot[d : d + 1, :]).astype(F32))
+            chosen = jnp.concatenate(hits, axis=0).astype(BF16)
+            pick[i] = chosen
+            rows = dot(chosen, gathered[i, 0:tokens_here, lanes])
+        else:
+            weight = table_rows(i)
+            weight_rows = jnp.concatenate(
+                [jnp.broadcast_to(weight[d : d + 1, :], (MAIN, tokens_here)) for d in range(peers)], axis=0
             )
-            for c in range(CORES):
-                weights.append(
-                    jnp.sum(jnp.where(row_ids == z * CORES + c, info, 0.0), axis=0, keepdims=True)
-                )
-        weight = jnp.concatenate(weights, axis=0)
-        named = weight > 0.0
-        before = dot(named.astype(F32).astype(BF16), earlier)
-        slot = jnp.where(named, before, -1.0)
-        extra_rows = lax.broadcasted_iota(jnp.int32, (MAIN, tokens_here), 0)
-        extra_slots = jnp.where(
-            lax.div(extra_rows, EXTRA) == within, MAIN + lax.rem(extra_rows, EXTRA), -2
-        ).astype(F32)
-        hits = []
-        for slots in (main_slots, extra_slots):
-            for d in range(peers):
-                hits.append((slots == slot[d : d + 1, :]).astype(F32))
-        chosen = jnp.concatenate(hits, axis=0)
-        weight_rows = jnp.concatenate(
-            [jnp.broadcast_to(weight[d : d + 1, :], (MAIN, tokens_here)) for d in range(peers)], axis=0
-        )
-        weighted = chosen * jnp.concatenate([weight_rows, weight_rows], axis=0)
-        pick[i] = chosen.astype(BF16)
-        weigh[i] = weighted.astype(BF16)
-        scale = jnp.sum(weighted, axis=1, keepdims=True)
-        chosen = chosen.astype(BF16)
-        main_count = peers * MAIN
-        for part in range(2):
-            lanes = slice(part * latent, (part + 1) * latent)
-            rows = dot(chosen, gathered[i, 0:tokens_here, lanes])
-            if part == 1:
-                rows = rows * scale
-            first = s * SET_ROWS + within * MAIN
-            send_rows[:, first : first + MAIN, lanes] = (
-                rows[:main_count].astype(BF16).reshape(peers, MAIN, latent)
-            )
-            extra = rows[main_count:]
-            if within > 0:
-                extra = extra + extra_sum[:, lanes]
-            if within < SET - 1:
-                extra_sum[:, lanes] = extra
-            else:
-                first = s * SET_ROWS + SET * MAIN
-                send_rows[:, first : first + MAIN, lanes] = extra.astype(BF16).reshape(peers, MAIN, latent)
+            chosen = pick[i]
+            weighted = chosen.astype(F32) * jnp.concatenate([weight_rows, weight_rows], axis=0)
+            weigh[i] = weighted.astype(BF16)
+            scale = jnp.sum(weighted, axis=1, keepdims=True)
+            rows = dot(chosen, gathered[i, 0:tokens_here, lanes]) * scale
+        first = s * SET_ROWS + within * MAIN
+        send_rows[:, first : first + MAIN, lanes] = rows[:main_count].astype(BF16).reshape(peers, MAIN, latent)
+        extra = rows[main_count:]
+        if within > 0:
+            extra = extra + extra_sum[:, lanes]
+        if within < SET - 1:
+            extra_sum[:, lanes] = extra
+        else:
+            first = s * SET_ROWS + SET * MAIN
+            send_rows[:, first : first + MAIN, lanes] = extra.astype(BF16).reshape(peers, MAIN, latent)
         count = MAIN if within < SET - 1 else 2 * MAIN
+        lanes = pl.ds(part * latent, latent)
 
         def start(j, carry):
-            slot_copy(j, s, within * MAIN, count).start()
+            slot_copy(j, s, within * MAIN, count, lanes).start()
             return carry
 
         lax.fori_loop(1, peers, start, 0)
-        own_slots(s, within * MAIN, count).start()
+        own_slots(s, within * MAIN, count, lanes).start()
 
     def side_copy(k, c, source):
         return pltpu.make_async_remote_copy(
@@ -290,9 +341,8 @@
             device_id_type=MESH,
         )
 
-    for way in range(2):
-        gather_copy(way, 0).start()
-    dispatch(0)
+    for part in range(2):
+        dispatch(0, part)
     near = sorted({1, groups - 1})
     for k in near:
         for c, source in enumerate((tokens_ref, cotan_ref)):
@@ -308,42 +358,65 @@
 
     sides[0, core] = jnp.where(core == 0, tokens_ref[...], cotan_ref[...])
     for step in range(1, half):
-        for way in range(2):
-            gather_copy(way, step - 1).wait_recv()
-            gather_copy(way, step).start()
-        for way in range(2):
-            dispatch(2 * step - 1 + way)
-    for way in range(2):
-        gather_copy(way, half - 1).wait_recv()
-    dispatch(ring - 1)
-
-    def back_copy(j, s):
+        for part in range(2):
+            for way in range(2):
+                gather_copy(way, step - 1, part).wait_recv()
+                if (way, part) in gather_pieces(step):
+                    gather_copy(way, step, part).start()
+            for way in range(2):
+                dispatch(2 * step - 1 + way, part)
+
+    back_pieces = [((SET - 1) * MAIN, 2 * MAIN)] + [(n * MAIN, MAIN) for n in range(SET - 2, -1, -1)]
+
+    def back_copy(j, s, n):
         d = peer(j)
-        rows = pl.ds(s * SET_ROWS, SET_ROWS)
+        first, count = back_pieces[n]
+        rows = pl.ds(s * SET_ROWS + first, count)
         return pltpu.make_async_remote_copy(
             src_ref=result_rows.at[d, rows],
             dst_ref=back_rows.at[place, rows],
-            send_sem=back_send.at[s, j],
-            recv_sem=back_recv.at[s, j],
+            send_sem=back_send.at[s, n, j],
+            recv_sem=back_recv.at[s, n, j],
             device_id=at_peer(d),
             device_id_type=MESH,
         )
 
-    def own_back(s):
-        rows = pl.ds(s * SET_ROWS, SET_ROWS)
-        return pltpu.make_async_copy(result_rows.at[place, rows], back_rows.at[place, rows], own_sem.at[1, s])
+    def own_back(s, n):
+        first, count = back_pieces[n]
+        rows = pl.ds(s * SET_ROWS + first, count)
+        return pltpu.make_async_copy(result_rows.at[place, rows], back_rows.at[place, rows], own_sem.at[1 + n, s])
 
     tile = min(256, hidden)
     wide = min(256, latent)
     count = peers * SET_ROWS
 
+    def send_back(s, n):
+        def start(j, carry):
+            back_copy(j, s, n).start()
+            return carry
+
+        lax.fori_loop(1, peers, start, 0)
+        own_back(s, n).start()
+
+    left_pieces = set()
+
+    def back_left(s, n):
+        def left(j, carry):
+            back_copy(j, s, n).wait_send()
+            return carry
+
+        left_pieces.add((s, n))
+        lax.fori_loop(1, peers, left, 0)
+
+    def slots_arrived(s):
+        def arrived(j, carry):
+            slot_copy(j, s, 0, SET_ROWS, all_lanes).wait_recv()
+            return carry
+
+        lax.fori_loop(1, peers, arrived, 0)
+        own_slots(s, 0, SET_ROWS, all_lanes).wait()
+
     def expert(s):
-        def arrived(j, carry):
-            slot_copy(j, s, 0, SET_ROWS).wait_recv()
-            return carry
-
-        lax.fori_loop(1, peers, arrived, 0)
-        own_slots(s, 0, SET_ROWS).wait()
         set_rows = slice(s * SET_ROWS, (s + 1) * SET_ROWS)
 
         def hidden_tile(h, carry):
@@ -378,22 +451,28 @@
 
         lax.fori_loop(0, latent // wide, latent_tile, 0)
 
-        def start(j, carry):
-            back_copy(j, s).start()
-            return carry
-
-        lax.fori_loop(1, peers, start, 0)
-        own_back(s).start()
-
+
+    for load in loads[4:]:
+        load.wait()
+    for s in range(sets - 1):
+        slots_arrived(s)
+        expert(s)
+    for way, part in gather_pieces(half - 1):
+        gather_copy(way, half - 1, part).wait_recv()
+    for part in range(2):
+        dispatch(ring - 1, part)
     for c in range(CORES):
         for k in near:
             side_arrived(k, c)
     if across > 1:
         for c in range(CORES):
             relay_copy(c).start()
-
-    for s in range(sets):
-        expert(s)
+    last_set = sets - 1
+    slots_arrived(last_set)
+    for s in range(last_set):
+        send_back(s, 0)
+    expert(last_set)
+    send_back(last_set, 0)
 
     share = hidden // groups
     all_rows = peers * sets * SET_ROWS
@@ -425,8 +504,11 @@
         grad_copy(k).start()
         return carry
 
-    lax.fori_loop(1, groups, other_share, 0)
-    gate_grad_ref[...], up_grad_ref[...], out_grad_ref[...] = weight_terms(0)
+    lax.fori_loop(1, groups - 1, other_share, 0)
+    back_left(last_set, 0)
+    send_back(last_set, 1)
+    send_back(last_set, 2)
+    lax.fori_loop(groups - 1, groups, other_share, 0)
 
     def combine(i):
         s, within = i // SET, i % SET
@@ -446,59 +528,71 @@
             parts.append(dot(matrix[i], rows, ROWS))
         return parts
 
-    def ring_copy(way, step):
-        lanes = pl.ds(way * latent, latent) if step == 0 else pl.ds(0, 2 * latent)
+    def ring_copy(way, step, part):
+        lanes = pl.ds(part * latent, latent)
         return pltpu.make_async_remote_copy(
             src_ref=ring_out.at[way, step, :, lanes],
             dst_ref=ring_in.at[way, step, :, lanes],
-            send_sem=ring_send.at[way, step],
-            recv_sem=ring_recv.at[way, step],
+            send_sem=ring_send.at[way, step, part],
+            recv_sem=ring_recv.at[way, step, part],
             device_id=on_ring(-1 if way == 0 else 1),
             device_id_type=MESH,
         )
 
-    def returned(s):
+    def ring_pieces(step):
+        pieces = [(way, 1 - way) for way in range(2)] if step > 0 else []
+        return pieces + [(way, way) for way in range(2)]
+
+    arrived_pieces = set()
+
+    def ready(i):
+        s = i // SET
+        n = SET - 1 - i % SET
+        if (s, n) in arrived_pieces:
+            return
+        arrived_pieces.add((s, n))
+
         def arrived(j, carry):
-            back_copy(j, s).wait_recv()
+            back_copy(j, s, n).wait_recv()
             return carry
 
         lax.fori_loop(1, peers, arrived, 0)
-        own_back(s).wait()
-
-    waiting = set(range(sets))
-
-    def ready(i):
-        if i // SET in waiting:
-            waiting.remove(i // SET)
-            returned(i // SET)
+        own_back(s, n).wait()
 
     ready(ring - 1)
     parts = combine(ring - 1)
-    for way in range(2):
-        ring_out[way, 0, :, way * latent : (way + 1) * latent] = parts[way].astype(BF16)
-        ring_copy(way, 0).start()
+    for way, part in ring_pieces(0):
+        ring_out[way, 0, :, part * latent : (part + 1) * latent] = parts[part].astype(BF16)
+        ring_copy(way, 0, part).start()
+    gate_grad_ref[...], up_grad_ref[...], out_grad_ref[...] = weight_terms(0)
+    back_left(last_set, 1)
+    back_left(last_set, 2)
+    send_back(last_set, 3)
+    for s in range(last_set):
+        for n in range(1, SET):
+            send_back(s, n)
     for step in range(1, half):
+        parts = []
         for way in range(2):
             i = 2 * (half - step) - 1 + way
             ready(i)
-            parts = combine(i)
-            ring_copy(way, step - 1).wait_recv()
-            for part in range(2):
-                lanes = slice(part * latent, (part + 1) * latent)
-                value = parts[part]
-                if step > 1 or part == way:
-                    value = value + ring_in[way, step - 1, :, lanes].astype(F32)
-                ring_out[way, step, :, lanes] = value.astype(BF16)
-            ring_copy(way, step).start()
+            parts.append(combine(i))
+        for way, part in ring_pieces(step):
+            lanes = slice(part * latent, (part + 1) * latent)
+            value = parts[way][part]
+            if (way, part) in ring_pieces(step - 1):
+                ring_copy(way, step - 1, part).wait_recv()
+                value = value + ring_in[way, step - 1, :, lanes].astype(F32)
+            ring_out[way, step, :, lanes] = value.astype(BF16)
+            ring_copy(way, step, part).start()
     ready(0)
     parts = combine(0)
-    for way in range(2):
-        ring_copy(way, half - 1).wait_recv()
     for part in range(2):
         lanes = slice(part * latent, (part + 1) * latent)
         value = parts[part]
         for way in range(2):
-            if half > 1 or way == part:
+            if (way, part) in ring_pieces(half - 1):
+                ring_copy(way, half - 1, part).wait_recv()
                 value = value + ring_in[way, half - 1, :, lanes].astype(F32)
         mid[:, lanes] = value.astype(BF16)
 
@@ -535,8 +629,10 @@
     for k, c in mates:
         late_copy(k, c).start()
     lates[0, core] = mid[:, late_lanes(0, core)]
-    mixed_ref[...] = dot(mid[:, 0:latent], up_ref[...], COLS).astype(BF16)
-    token_grad_ref[...] = dot(mid[:, latent:], down_ref[...], COLS).astype(BF16)
+    mixed_ref[...] = dot(mid[:, 0:latent], up_ref[...], COLS)
+    token_grad_ref[...] = dot(mid[:, latent:], down_ref[...], COLS)
+    stores[0].start()
+    stores[1].start()
 
     side_arrived(0, 1 - core)
     if across > 1:
@@ -545,11 +641,11 @@
     for k, c in mates:
         late_arrived(k, c)
     both = groups * CORES * tokens_here
+    late_columns = lates[...].reshape(both, block).astype(F32).T.astype(BF16)
 
     def term_rows(k):
         cols = pl.ds(pl.multiple_of(lax.rem(lax.div(me, ring * CORES) + k, columns) * column_rows, column_rows), column_rows)
-        term = dot(lates[...].reshape(both, block), sides[:, :, :, cols].reshape(both, column_rows), ROWS)
-        return term.T
+        return dot(late_columns, sides[:, :, :, cols].reshape(both, column_rows)).T
 
     def x_copy(k):
         return pltpu.make_async_remote_copy(
@@ -565,6 +661,13 @@
         x_out[k] = term_rows(k).astype(BF16)
         x_copy(k).start()
     total = term_rows(0)
+    for k in range(1, groups):
+        grad_copy(k).wait_recv()
+        gate_grad_ref[...] += grads_in[k, 0:latent, 0:share].astype(F32)
+        up_grad_ref[...] += grads_in[k, 0:latent, share:].astype(F32)
+        out_grad_ref[...] += grads_in[k, latent:, :].astype(F32)
+    for store in stores[4:]:
+        store.start()
     for k in range(1, columns):
         x_copy(k).wait_recv()
         total = total + x_in[k].astype(F32)
@@ -603,18 +706,14 @@
         last_copy(k, c, core).start()
     last_in[0, core] = last_out[core]
 
-    for k in range(1, groups):
-        grad_copy(k).wait_recv()
-        gate_grad_ref[...] += grads_in[k, 0:latent, 0:share].astype(F32)
-        up_grad_ref[...] += grads_in[k, 0:latent, share:].astype(F32)
-        out_grad_ref[...] += grads_in[k, latent:, :].astype(F32)
-
     for k, c in mates:
         last_copy(k, c, c).wait_recv()
     for k in range(groups):
         lanes = pl.ds(pl.multiple_of(lax.rem(my_group + groups - k, groups) * block, block), block)
         down_grad_ref[:, lanes] = last_in[k, 0]
         up_proj_grad_ref[:, lanes] = last_in[k, 1]
+    stores[2].start()
+    stores[3].start()
 
     for k in near:
         for c in range(CORES):
@@ -631,20 +730,25 @@
     for r in range(1, ring):
         z_copy(r).wait_send()
 
-    for way in range(2):
-        for step in range(half):
-            gather_copy(way, step).wait_send()
-            ring_copy(way, step).wait_send()
+    for step in range(half):
+        for way, part in gather_pieces(step):
+            gather_copy(way, step, part).wait_send()
+        for way, part in ring_pieces(step):
+            ring_copy(way, step, part).wait_send()
 
     def sent(j, carry):
         for s in range(sets):
-            slot_copy(j, s, 0, SET_ROWS).wait_send()
-            back_copy(j, s).wait_send()
+            slot_copy(j, s, 0, SET_ROWS, all_lanes).wait_send()
+            for n in range(SET):
+                if (s, n) not in left_pieces:
+                    back_copy(j, s, n).wait_send()
         return carry
 
     lax.fori_loop(1, peers, sent, 0)
     for k in range(1, groups):
         grad_copy(k).wait_send()
+    for store in stores:
+        store.wait()
 
 
 def layer(ring, routes, gates, tokens, cotan, down, up, gate_weight, up_weight, out_weight):
@@ -664,21 +768,27 @@
     last_rows = features // experts
     ring_rows = last_rows * CORES
     vmem = pl.BlockSpec(memory_space=pltpu.VMEM)
+    anywhere = pl.BlockSpec(memory_space=pl.ANY)
     dma = pltpu.SemaphoreType.DMA
+    arrays = (tokens, cotan, down, up, gate_weight, up_weight, out_weight)
+    results = (
+        jax.ShapeDtypeStruct((count, features), F32),
+        jax.ShapeDtypeStruct((count, features), F32),
+        jax.ShapeDtypeStruct((last_rows, latent), F32),
+        jax.ShapeDtypeStruct((last_rows, latent), F32),
+        jax.ShapeDtypeStruct((latent, share), F32),
+        jax.ShapeDtypeStruct((latent, share), F32),
+        jax.ShapeDtypeStruct((share, latent), F32),
+    )
     return pl.pallas_call(
         partial(layer_kernel, ring),
-        out_shape=(
-            jax.ShapeDtypeStruct((count, features), BF16),
-            jax.ShapeDtypeStruct((count, features), BF16),
-            jax.ShapeDtypeStruct((last_rows, latent), F32),
-            jax.ShapeDtypeStruct((last_rows, latent), F32),
-            jax.ShapeDtypeStruct((latent, share), F32),
-            jax.ShapeDtypeStruct((latent, share), F32),
-            jax.ShapeDtypeStruct((share, latent), F32),
-        ),
-        in_specs=[vmem] * 9,
-        out_specs=(vmem,) * 7,
-        scratch_shapes=[
+        out_shape=results,
+        in_specs=[vmem] * 2 + [anywhere] * 7,
+        out_specs=(anywhere,) * 7,
+        scratch_shapes=[pltpu.VMEM(a.shape, a.dtype) for a in arrays + results]
+        + [
+            dma((len(arrays),)),
+            dma((len(results),)),
             pltpu.VMEM((count, 2 * latent), BF16),
             pltpu.VMEM((groups, CORES, count, features), BF16),
             pltpu.VMEM((groups, CORES, count, block), BF16),
@@ -704,15 +814,15 @@
             pltpu.VMEM((2, half, count, 2 * latent), BF16),
             pltpu.VMEM((groups, latent + share, 2 * share), BF16),
             pltpu.VMEM((groups, latent + share, 2 * share), BF16),
-            dma((2, half)),
-            dma((2, half)),
+            dma((2, half, 2)),
+            dma((2, half, 2)),
             dma((sets, peers)),
             dma((sets, peers)),
-            dma((sets, peers)),
-            dma((sets, peers)),
-            dma((2, sets)),
-            dma((2, half)),
-            dma((2, half)),
+            dma((sets, SET, peers)),
+            dma((sets, SET, peers)),
+            dma((1 + SET, sets)),
+            dma((2, half, 2)),
+            dma((2, half, 2)),
             dma((groups,)),
             dma((groups,)),
             dma((groups, CORES)),
@@ -758,6 +868,7 @@
         up_weight[0],
         out_weight[0],
     )
+    mixed, grad_tokens = mixed.astype(BF16), grad_tokens.astype(BF16)
     return mixed, grad_tokens, down_grad, up_proj_grad, gate_grad[None], up_grad[None], out_grad[None]
 
 

time: 142 us -> 125 us (0.88)
  Pallas kernels: 134 us -> 117 us
  local copies, waits for them, and re-layouts: 7.54 us -> 3.66 us
  other arithmetic: 0 us -> 3.09 us
    pallas_call x1, Pallas kernels: 134 us -> 117 us  [layer(): pl.pallas_call(partial(layer_kernel, ring), out_shape=results, in_specs=[...]
    unnamed x17, local copies, waits for them, and re-layouts: 7.54 us -> 3.66 us
    convert_element_type x0 -> x2, other arithmetic: none -> 3.09 us  [shards(): mixed, grad_tokens = (mixed.astype(BF16), grad_tokens.astype(BF16))]
where the time goes in v3:
time: 125 us
  Pallas kernels  117 us (94%)
  local copies, waits for them, and re-layouts  3.66 us (3%)
  other arithmetic  3.09 us (2%)
    pallas_call x1, Pallas kernels, layer(): pl.pallas_call(partial(layer_kernel, ring), out_shape=results, in_specs=[...  117 us
    unnamed x17, local copies, waits for them, and re-layouts  3.66 us
    convert_element_type x2, other arithmetic, shards(): mixed, grad_tokens = (mixed.astype(BF16), grad_tokens.astype(BF16))  3.09 us

profile of v3, /device:TPU:1, one launch (start us, length us, event | category | flops | bytes accessed | tf_op | source)
XLA Modules:
  0.0 124.7 jit_solution(14374632597329910473)
XLA Ops:
  0.6 117.2 %layer.1 = (f32[128,2048]{1,0:T(8,128)}, f32[128,2048]{1,0:T(8,128)}, f32[32,512]{1,0:T(8,128)}, f32[32,512]{1,0:T(8,128)}, f32[512,256]{1,0:T(8,128)}, /*index=5*/f32[512,256]{1,0:T(8,128)}, f32[256,512]{1,0:T(8,128)}) custom-call(s32[8,128]{1,0:T(8,128)} %bitcast.14, f32[8,128]{1,0:T(8,128)} %bitcast.15, bf16[128,2048]{1,0:T(8,128)(2,1)} %tokens_hbm.1, ...), custom_call_target="tpu_custom_call" | custom-call | tf_op jit(solution)/shard_map/layer/pallas_call | solution.py:783
  117.9 0.0 copy-start
  117.9 0.0 copy-start.5
  117.9 0.0 copy-start.4
  117.9 0.0 copy-start.3
  117.9 0.0 copy-start.2
  117.9 2.2 %convert_element_type.6 = bf16[128,2048]{1,0:T(8,128)(2,1)} convert(f32[128,2048]{1,0:T(8,128)} %get-tuple-element.14) | non-fusion elementwise | flops 262144 | bytes 1572864 | tf_op jit(solution)/shard_map/convert_element_type | solution.py:871
  120.1 0.0 copy-done
  120.2 0.0 copy-start.1
  120.2 0.9 convert_element_type.7
  121.0 0.0 copy-done.5
  121.0 0.6 copy.21
  121.6 0.0 copy-done.4
  121.6 0.6 copy.22
  122.3 0.0 copy-done.3
  122.3 0.8 copy.23
  123.1 0.0 copy-done.2
  123.1 0.8 copy.24
  123.9 0.0 copy-done.1
  123.9 0.8 copy.25
Async XLA Ops:
  117.9 2.3 %copy-start = (f32[128,2048]{1,0:T(8,128)S(1)}, f32[128,2048]{1,0:T(8,128)}, u32[]{:S(2)}) copy-start(f32[128,2048]{1,0:T(8,128)} %get-tuple-element.15) | copy-start | bytes 3145732
  117.9 3.1 %copy-start.5 = (f32[32,512]{1,0:T(8,128)S(1)}, f32[32,512]{1,0:T(8,128)}, u32[]{:S(2)}) copy-start(f32[32,512]{1,0:T(8,128)} %get-tuple-element.30) | copy-start | bytes 196612
  117.9 3.8 %copy-start.4 = (f32[32,512]{1,0:T(8,128)S(1)}, f32[32,512]{1,0:T(8,128)}, u32[]{:S(2)}) copy-start(f32[32,512]{1,0:T(8,128)} %get-tuple-element.31) | copy-start | bytes 196612
  117.9 4.4 %copy-start.3 = (f32[512,256]{1,0:T(8,128)S(1)}, f32[512,256]{1,0:T(8,128)}, u32[]{:S(2)}) copy-start(f32[512,256]{1,0:T(8,128)} %get-tuple-element.18) | copy-start | bytes 1572868
  117.9 5.2 %copy-start.2 = (f32[512,256]{1,0:T(8,128)S(1)}, f32[512,256]{1,0:T(8,128)}, u32[]{:S(2)}) copy-start(f32[512,256]{1,0:T(8,128)} %get-tuple-element.19) | copy-start | bytes 1572868
  120.2 3.7 %copy-start.1 = (f32[256,512]{1,0:T(8,128)S(1)}, f32[256,512]{1,0:T(8,128)}, u32[]{:S(2)}) copy-start(f32[256,512]{1,0:T(8,128)} %get-tuple-element.20) | copy-start | bytes 1572868

commit v4 on v3

--- a/solution.py
+++ b/solution.py
@@ -40,8 +40,7 @@
     ow_hbm,
     mixed_hbm,
     token_grad_hbm,
-    down_grad_hbm,
-    up_proj_grad_hbm,
+    proj_hbm,
     gate_grad_hbm,
     up_grad_hbm,
     out_grad_hbm,
@@ -54,8 +53,6 @@
     ow_ref,
     mixed_ref,
     token_grad_ref,
-    down_grad_ref,
-    up_proj_grad_ref,
     gate_grad_ref,
     up_grad_ref,
     out_grad_ref,
@@ -70,7 +67,6 @@
     z_out,
     z_in,
     last_out,
-    last_in,
     gathered,
     send_rows,
     expert_rows,
@@ -86,6 +82,7 @@
     ring_in,
     grads_out,
     grads_in,
+    grads_half,
     gather_send,
     gather_recv,
     slot_send,
@@ -97,6 +94,8 @@
     ring_recv,
     grad_send,
     grad_recv,
+    half_send,
+    half_recv,
     side_send,
     side_recv,
     relay_send,
@@ -169,15 +168,13 @@
             (
                 (mixed_ref, mixed_hbm),
                 (token_grad_ref, token_grad_hbm),
-                (down_grad_ref, down_grad_hbm),
-                (up_proj_grad_ref, up_proj_grad_hbm),
                 (gate_grad_ref, gate_grad_hbm),
                 (up_grad_ref, up_grad_hbm),
                 (out_grad_ref, out_grad_hbm),
             )
         )
     ]
-    for load in loads[:4]:
+    for load in loads[:2]:
         load.start()
 
     expert_ids = lax.broadcasted_iota(jnp.int32, (experts, tokens_here), 0)
@@ -210,6 +207,8 @@
 
     loads[0].wait()
     loads[1].wait()
+    for load in loads[2:4]:
+        load.start()
     gathered[0, 0:tokens_here, 0:latent] = dot(tokens_ref[...], down_ref[...]).astype(BF16)
     pl.semaphore_wait(barrier, (ring - 1) + (peers - 1) + len(mates))
     for way in range(2):
@@ -229,22 +228,32 @@
     row_ids = lax.broadcasted_iota(jnp.int32, (per_column, tokens_here), 0)
     main_slots = lax.broadcasted_iota(jnp.int32, (MAIN, tokens_here), 0).astype(F32)
 
-    def slot_copy(j, s, first, count, lanes):
+    last_set = sets - 1
+    near_rows = (SET - 1) * MAIN
+    chunks = [(s * SET_ROWS, SET_ROWS) for s in range(last_set)] + [
+        (last_set * SET_ROWS, near_rows),
+        (last_set * SET_ROWS + near_rows, SET_ROWS - near_rows),
+    ]
+
+    def chunk_of(i):
+        return i // SET + (1 if i == ring - 1 else 0)
+
+    def slot_copy(j, chunk, first, count, lanes):
         d = peer(j)
-        rows = pl.ds(s * SET_ROWS + first, count)
+        rows = pl.ds(first, count)
         return pltpu.make_async_remote_copy(
             src_ref=send_rows.at[d, rows, lanes],
             dst_ref=expert_rows.at[place, rows, lanes],
-            send_sem=slot_send.at[s, j],
-            recv_sem=slot_recv.at[s, j],
+            send_sem=slot_send.at[chunk, j],
+            recv_sem=slot_recv.at[chunk, j],
             device_id=at_peer(d),
             device_id_type=MESH,
         )
 
-    def own_slots(s, first, count, lanes):
-        rows = pl.ds(s * SET_ROWS + first, count)
+    def own_slots(chunk, first, count, lanes):
+        rows = pl.ds(first, count)
         return pltpu.make_async_copy(
-            send_rows.at[place, rows, lanes], expert_rows.at[place, rows, lanes], own_sem.at[0, s]
+            send_rows.at[place, rows, lanes], expert_rows.at[place, rows, lanes], own_sem.at[0, chunk]
         )
 
     all_lanes = pl.ds(0, 2 * latent)
@@ -302,11 +311,11 @@
         lanes = pl.ds(part * latent, latent)
 
         def start(j, carry):
-            slot_copy(j, s, within * MAIN, count, lanes).start()
+            slot_copy(j, chunk_of(i), s * SET_ROWS + within * MAIN, count, lanes).start()
             return carry
 
         lax.fori_loop(1, peers, start, 0)
-        own_slots(s, within * MAIN, count, lanes).start()
+        own_slots(chunk_of(i), s * SET_ROWS + within * MAIN, count, lanes).start()
 
     def side_copy(k, c, source):
         return pltpu.make_async_remote_copy(
@@ -388,8 +397,6 @@
 
     tile = min(256, hidden)
     wide = min(256, latent)
-    count = peers * SET_ROWS
-
     def send_back(s, n):
         def start(j, carry):
             back_copy(j, s, n).start()
@@ -398,26 +405,18 @@
         lax.fori_loop(1, peers, start, 0)
         own_back(s, n).start()
 
-    left_pieces = set()
-
-    def back_left(s, n):
-        def left(j, carry):
-            back_copy(j, s, n).wait_send()
+    def slots_arrived(chunk):
+        def arrived(j, carry):
+            slot_copy(j, chunk, *chunks[chunk], all_lanes).wait_recv()
             return carry
 
-        left_pieces.add((s, n))
-        lax.fori_loop(1, peers, left, 0)
-
-    def slots_arrived(s):
-        def arrived(j, carry):
-            slot_copy(j, s, 0, SET_ROWS, all_lanes).wait_recv()
-            return carry
-
         lax.fori_loop(1, peers, arrived, 0)
-        own_slots(s, 0, SET_ROWS, all_lanes).wait()
-
-    def expert(s):
-        set_rows = slice(s * SET_ROWS, (s + 1) * SET_ROWS)
+        own_slots(chunk, *chunks[chunk], all_lanes).wait()
+
+    def expert(chunk):
+        first, per_peer = chunks[chunk]
+        set_rows = slice(first, first + per_peer)
+        count = peers * per_peer
 
         def hidden_tile(h, carry):
             cols = pl.ds(pl.multiple_of(h * tile, tile), tile)
@@ -428,7 +427,7 @@
             grad_act = dot(grad_in, ow_ref[cols, :], COLS)
             sig = 1.0 / (1.0 + jnp.exp(-pre_gate))
             swish = pre_gate * sig
-            shape = (peers, SET_ROWS, tile)
+            shape = (peers, per_peer, tile)
             act[:, set_rows, cols] = (swish * pre_up).astype(BF16).reshape(shape)
             grad_gate[:, set_rows, cols] = (
                 (grad_act * pre_up * (sig * (1.0 + pre_gate * (1.0 - sig)))).astype(BF16).reshape(shape)
@@ -441,7 +440,7 @@
         def latent_tile(n, carry):
             cols = pl.ds(pl.multiple_of(n * wide, wide), wide)
             later = pl.ds(pl.multiple_of(latent + n * wide, wide), wide)
-            shape = (peers, SET_ROWS, wide)
+            shape = (peers, per_peer, wide)
             out = dot(act[:, set_rows, :].reshape(count, hidden), ow_ref[:, cols])
             result_rows[:, set_rows, cols] = out.astype(BF16).reshape(shape)
             back = dot(grad_gate[:, set_rows, :].reshape(count, hidden), gw_ref[cols, :], COLS)
@@ -454,24 +453,25 @@
 
     for load in loads[4:]:
         load.wait()
-    for s in range(sets - 1):
-        slots_arrived(s)
-        expert(s)
+    for chunk in range(last_set):
+        slots_arrived(chunk)
+        expert(chunk)
     for way, part in gather_pieces(half - 1):
         gather_copy(way, half - 1, part).wait_recv()
     for part in range(2):
         dispatch(ring - 1, part)
+    slots_arrived(last_set)
+    expert(last_set)
     for c in range(CORES):
         for k in near:
             side_arrived(k, c)
     if across > 1:
         for c in range(CORES):
             relay_copy(c).start()
-    last_set = sets - 1
-    slots_arrived(last_set)
+    slots_arrived(last_set + 1)
     for s in range(last_set):
         send_back(s, 0)
-    expert(last_set)
+    expert(last_set + 1)
     send_back(last_set, 0)
 
     share = hidden // groups
@@ -501,14 +501,27 @@
         grads_out[k, 0:latent, 0:share] = gate_term.astype(BF16)
         grads_out[k, 0:latent, share:] = up_term.astype(BF16)
         grads_out[k, latent:, :] = out_term.astype(BF16)
-        grad_copy(k).start()
         return carry
 
-    lax.fori_loop(1, groups - 1, other_share, 0)
-    back_left(last_set, 0)
+    half_rows = (latent + share) // 2
+
+    def pass_copy(way):
+        return pltpu.make_async_remote_copy(
+            src_ref=grads_out.at[across, pl.ds(way * half_rows, half_rows)],
+            dst_ref=grads_half.at[way],
+            send_sem=half_send.at[way],
+            recv_sem=half_recv.at[way],
+            device_id=group_at(near[way]),
+            device_id_type=MESH,
+        )
+
+    if across > 1:
+        lax.fori_loop(across, across + 1, other_share, 0)
+        for way in range(2):
+            pass_copy(way).start()
     send_back(last_set, 1)
     send_back(last_set, 2)
-    lax.fori_loop(groups - 1, groups, other_share, 0)
+    lax.fori_loop(0, len(near), lambda n, carry: other_share(1 + (groups - 2) * n, carry), 0)
 
     def combine(i):
         s, within = i // SET, i % SET
@@ -565,8 +578,12 @@
         ring_out[way, 0, :, part * latent : (part + 1) * latent] = parts[part].astype(BF16)
         ring_copy(way, 0, part).start()
     gate_grad_ref[...], up_grad_ref[...], out_grad_ref[...] = weight_terms(0)
-    back_left(last_set, 1)
-    back_left(last_set, 2)
+    for way, k in enumerate(near):
+        if across > 1:
+            pass_copy(way).wait_recv()
+            rows = slice(way * half_rows, (way + 1) * half_rows)
+            grads_out[k, rows, :] = (grads_out[k, rows, :].astype(F32) + grads_half[way].astype(F32)).astype(BF16)
+        grad_copy(k).start()
     send_back(last_set, 3)
     for s in range(last_set):
         for n in range(1, SET):
@@ -657,16 +674,16 @@
             device_id_type=MESH,
         )
 
-    for k in range(1, columns):
+    for k in sorted(range(1, columns), key=lambda k: -min(k, columns - k)):
         x_out[k] = term_rows(k).astype(BF16)
         x_copy(k).start()
     total = term_rows(0)
-    for k in range(1, groups):
+    for k in near:
         grad_copy(k).wait_recv()
         gate_grad_ref[...] += grads_in[k, 0:latent, 0:share].astype(F32)
         up_grad_ref[...] += grads_in[k, 0:latent, share:].astype(F32)
         out_grad_ref[...] += grads_in[k, latent:, :].astype(F32)
-    for store in stores[4:]:
+    for store in stores[2:]:
         store.start()
     for k in range(1, columns):
         x_copy(k).wait_recv()
@@ -692,28 +709,40 @@
         total = total + z_in[r].astype(F32)
     last_out[...] = total.reshape(CORES, last_rows, block)
 
-    def last_copy(k, c, slot):
+    def group_lanes(k):
+        return pl.ds(pl.multiple_of(lax.rem(my_group + groups - k, groups) * block, block), block)
+
+    def last_copy(k, c):
         return pltpu.make_async_remote_copy(
             src_ref=last_out.at[c],
-            dst_ref=last_in.at[k, slot],
+            dst_ref=proj_hbm.at[core, :, group_lanes(0)],
             send_sem=last_send.at[k, c],
-            recv_sem=last_recv.at[k, slot],
+            recv_sem=last_recv.at[k, core],
             device_id=mate(k, c),
             device_id_type=MESH,
         )
 
+    def last_arrived(k, c):
+        pltpu.make_async_remote_copy(
+            src_ref=last_out.at[c],
+            dst_ref=proj_hbm.at[c, :, group_lanes(k)],
+            send_sem=last_send.at[k, c],
+            recv_sem=last_recv.at[k, c],
+            device_id=mate(k, c),
+            device_id_type=MESH,
+        ).wait_recv()
+
+    own_last = pltpu.make_async_copy(
+        last_out.at[core], proj_hbm.at[core, :, group_lanes(0)], last_recv.at[0, core]
+    )
+
     for k, c in mates:
-        last_copy(k, c, core).start()
-    last_in[0, core] = last_out[core]
-
+        last_copy(k, c).start()
+    own_last.start()
+
+    own_last.wait()
     for k, c in mates:
-        last_copy(k, c, c).wait_recv()
-    for k in range(groups):
-        lanes = pl.ds(pl.multiple_of(lax.rem(my_group + groups - k, groups) * block, block), block)
-        down_grad_ref[:, lanes] = last_in[k, 0]
-        up_proj_grad_ref[:, lanes] = last_in[k, 1]
-    stores[2].start()
-    stores[3].start()
+        last_arrived(k, c)
 
     for k in near:
         for c in range(CORES):
@@ -724,7 +753,7 @@
             relay_copy(c).wait_send()
     for k, c in mates:
         late_copy(k, c).wait_send()
-        last_copy(k, c, core).wait_send()
+        last_copy(k, c).wait_send()
     for k in range(1, columns):
         x_copy(k).wait_send()
     for r in range(1, ring):
@@ -737,16 +766,19 @@
             ring_copy(way, step, part).wait_send()
 
     def sent(j, carry):
+        for chunk in range(len(chunks)):
+            slot_copy(j, chunk, *chunks[chunk], all_lanes).wait_send()
         for s in range(sets):
-            slot_copy(j, s, 0, SET_ROWS, all_lanes).wait_send()
             for n in range(SET):
-                if (s, n) not in left_pieces:
-                    back_copy(j, s, n).wait_send()
+                back_copy(j, s, n).wait_send()
         return carry
 
     lax.fori_loop(1, peers, sent, 0)
-    for k in range(1, groups):
+    for k in near:
         grad_copy(k).wait_send()
+    if across > 1:
+        for way in range(2):
+            pass_copy(way).wait_send()
     for store in stores:
         store.wait()
 
@@ -774,8 +806,7 @@
     results = (
         jax.ShapeDtypeStruct((count, features), F32),
         jax.ShapeDtypeStruct((count, features), F32),
-        jax.ShapeDtypeStruct((last_rows, latent), F32),
-        jax.ShapeDtypeStruct((last_rows, latent), F32),
+        jax.ShapeDtypeStruct((CORES, last_rows, latent), F32),
         jax.ShapeDtypeStruct((latent, share), F32),
         jax.ShapeDtypeStruct((latent, share), F32),
         jax.ShapeDtypeStruct((share, latent), F32),
@@ -784,11 +815,11 @@
         partial(layer_kernel, ring),
         out_shape=results,
         in_specs=[vmem] * 2 + [anywhere] * 7,
-        out_specs=(anywhere,) * 7,
-        scratch_shapes=[pltpu.VMEM(a.shape, a.dtype) for a in arrays + results]
+        out_specs=(anywhere,) * len(results),
+        scratch_shapes=[pltpu.VMEM(a.shape, a.dtype) for a in arrays + results[:2] + results[3:]]
         + [
             dma((len(arrays),)),
-            dma((len(results),)),
+            dma((len(results) - 1,)),
             pltpu.VMEM((count, 2 * latent), BF16),
             pltpu.VMEM((groups, CORES, count, features), BF16),
             pltpu.VMEM((groups, CORES, count, block), BF16),
@@ -798,7 +829,6 @@
             pltpu.VMEM((ring, ring_rows, block), BF16),
             pltpu.VMEM((ring, ring_rows, block), BF16),
             pltpu.VMEM((CORES, last_rows, block), F32),
-            pltpu.VMEM((groups, CORES, last_rows, block), F32),
             pltpu.VMEM((ring, count + MAIN, 2 * latent), BF16),
             pltpu.VMEM((peers, rows, 2 * latent), BF16),
             pltpu.VMEM((peers, rows, 2 * latent), BF16),
@@ -814,17 +844,20 @@
             pltpu.VMEM((2, half, count, 2 * latent), BF16),
             pltpu.VMEM((groups, latent + share, 2 * share), BF16),
             pltpu.VMEM((groups, latent + share, 2 * share), BF16),
+            pltpu.VMEM((2, (latent + share) // 2, 2 * share), BF16),
             dma((2, half, 2)),
             dma((2, half, 2)),
-            dma((sets, peers)),
-            dma((sets, peers)),
+            dma((sets + 1, peers)),
+            dma((sets + 1, peers)),
             dma((sets, SET, peers)),
             dma((sets, SET, peers)),
-            dma((1 + SET, sets)),
+            dma((1 + SET, sets + 1)),
             dma((2, half, 2)),
             dma((2, half, 2)),
             dma((groups,)),
             dma((groups,)),
+            dma((2,)),
+            dma((2,)),
             dma((groups, CORES)),
             dma((groups, CORES)),
             dma((CORES,)),
@@ -856,7 +889,7 @@
     latent_up,
     grad_mixed,
 ):
-    mixed, grad_tokens, down_grad, up_proj_grad, gate_grad, up_grad, out_grad = layer(
+    mixed, grad_tokens, proj_grads, gate_grad, up_grad, out_grad = layer(
         ring,
         routes.T,
         gate_values.T,
@@ -869,7 +902,7 @@
         out_weight[0],
     )
     mixed, grad_tokens = mixed.astype(BF16), grad_tokens.astype(BF16)
-    return mixed, grad_tokens, down_grad, up_proj_grad, gate_grad[None], up_grad[None], out_grad[None]
+    return mixed, grad_tokens, proj_grads[0], proj_grads[1], gate_grad[None], up_grad[None], out_grad[None]
 
 
 def solution(mesh, ring=RING):

time: 125 us -> 123 us (0.984)
  Pallas kernels: 117 us -> 115 us
    pallas_call x1, Pallas kernels: 117 us -> 115 us  [layer(): pl.pallas_call(partial(layer_kernel, ring), out_shape=results, in_specs=[...]
    squeeze x0 -> x1, local copies, waits for them, and re-layouts: none -> 1.59 us  [shards(): proj_grads[1]]
    unnamed x17 -> x11, local copies, waits for them, and re-layouts: 3.66 us -> 2.4 us
where the time goes in v4:
time: 123 us; the launch traced here: 122 us
  Pallas kernels  115 us (93%)
  local copies, waits for them, and re-layouts  3.98 us (3%)
  other arithmetic  3.09 us (3%)
    pallas_call x1, Pallas kernels, layer(): pl.pallas_call(partial(layer_kernel, ring), out_shape=results, in_specs=[...  115 us
    convert_element_type x2, other arithmetic, shards(): mixed, grad_tokens = (mixed.astype(BF16), grad_tokens.astype(BF16))  3.09 us

profile of v4, /device:TPU:1, one launch (start us, length us, event | category | flops | bytes accessed | tf_op | source)
XLA Modules:
  0.0 122.4 jit_solution(16560604475102718200)
XLA Ops:
  0.6 114.7 %layer.1 = (f32[128,2048]{1,0:T(8,128)}, f32[128,2048]{1,0:T(8,128)}, f32[2,32,512]{2,1,0:T(8,128)}, f32[512,256]{1,0:T(8,128)}, f32[512,256]{1,0:T(8,128)}, /*index=5*/f32[256,512]{1,0:T(8,128)}) custom-call(s32[8,128]{1,0:T(8,128)} %bitcast.18, f32[8,128]{1,0:T(8,128)} %bitcast.19, bf16[128,2048]{1,0:T(8,128)(2,1)} %tokens_hbm.1, ...), custom_call_target="tpu_custom_call" | custom-call | tf_op jit(solution)/shard_map/layer/pallas_call | solution.py:814
  115.3 0.0 copy-start
  115.3 0.0 copy-start.3
  115.3 0.0 copy-start.2
  115.3 2.2 %convert_element_type.6 = bf16[128,2048]{1,0:T(8,128)(2,1)} convert(f32[128,2048]{1,0:T(8,128)} %get-tuple-element.13) | non-fusion elementwise | flops 262144 | bytes 1572864 | tf_op jit(solution)/shard_map/convert_element_type | solution.py:904
  117.6 0.0 copy-start.1
  117.6 1.6 %slice_bitcast_fusion = (f32[32,512]{1,0:T(8,128)}, f32[32,512]{1,0:T(8,128)}) fusion(f32[2,32,512]{2,1,0:T(8,128)} %get-tuple-element.15), kind=kLoop, calls=%fused_computation | loop fusion | bytes 262144 | tf_op jit(solution)/shard_map/squeeze | solution.py:905
  119.1 0.0 copy-done
  119.1 0.9 convert_element_type.7
  120.0 0.0 copy-done.3
  120.0 0.8 copy.19
  120.8 0.0 copy-done.2
  120.8 0.8 copy.20
  121.6 0.0 copy-done.1
  121.6 0.8 copy.21
Async XLA Ops:
  115.3 3.9 %copy-start = (f32[128,2048]{1,0:T(8,128)S(1)}, f32[128,2048]{1,0:T(8,128)}, u32[]{:S(2)}) copy-start(f32[128,2048]{1,0:T(8,128)} %get-tuple-element.14) | copy-start | bytes 3145732
  115.3 4.7 %copy-start.3 = (f32[512,256]{1,0:T(8,128)S(1)}, f32[512,256]{1,0:T(8,128)}, u32[]{:S(2)}) copy-start(f32[512,256]{1,0:T(8,128)} %get-tuple-element.16) | copy-start | bytes 1572868
  115.3 5.5 %copy-start.2 = (f32[512,256]{1,0:T(8,128)S(1)}, f32[512,256]{1,0:T(8,128)}, u32[]{:S(2)}) copy-start(f32[512,256]{1,0:T(8,128)} %get-tuple-element.17) | copy-start | bytes 1572868
  117.6 4.0 %copy-start.1 = (f32[256,512]{1,0:T(8,128)S(1)}, f32[256,512]{1,0:T(8,128)}, u32[]{:S(2)}) copy-start(f32[256,512]{1,0:T(8,128)} %get-tuple-element.18) | copy-start | bytes 1572868

commit v5 on v4

--- a/solution.py
+++ b/solution.py
@@ -61,6 +61,7 @@
     mid,
     sides,
     lates,
+    term_sum,
     x_out,
     x_in,
     x_sum,
@@ -473,6 +474,12 @@
         send_back(s, 0)
     expert(last_set + 1)
     send_back(last_set, 0)
+    send_back(last_set, 1)
+    send_back(last_set, 2)
+    send_back(last_set, 3)
+    for s in range(last_set):
+        for n in range(1, SET):
+            send_back(s, n)
 
     share = hidden // groups
     all_rows = peers * sets * SET_ROWS
@@ -519,8 +526,6 @@
         lax.fori_loop(across, across + 1, other_share, 0)
         for way in range(2):
             pass_copy(way).start()
-    send_back(last_set, 1)
-    send_back(last_set, 2)
     lax.fori_loop(0, len(near), lambda n, carry: other_share(1 + (groups - 2) * n, carry), 0)
 
     def combine(i):
@@ -584,10 +589,6 @@
             rows = slice(way * half_rows, (way + 1) * half_rows)
             grads_out[k, rows, :] = (grads_out[k, rows, :].astype(F32) + grads_half[way].astype(F32)).astype(BF16)
         grad_copy(k).start()
-    send_back(last_set, 3)
-    for s in range(last_set):
-        for n in range(1, SET):
-            send_back(s, n)
     for step in range(1, half):
         parts = []
         for way in range(2):
@@ -602,6 +603,36 @@
                 value = value + ring_in[way, step - 1, :, lanes].astype(F32)
             ring_out[way, step, :, lanes] = value.astype(BF16)
             ring_copy(way, step, part).start()
+    block = latent // groups
+    features = tokens_ref.shape[1]
+    column_rows = features // columns
+    ring_rows = column_rows // ring
+    last_rows = ring_rows // CORES
+
+    def late_lanes(k, c):
+        start = latent * (1 - c) + block * lax.rem(my_group + k, groups)
+        return pl.ds(pl.multiple_of(start, block), block)
+
+    def late_copy(k, c):
+        return pltpu.make_async_remote_copy(
+            src_ref=mid.at[:, late_lanes(k, c)],
+            dst_ref=lates.at[k, core],
+            send_sem=late_send.at[k, c],
+            recv_sem=late_recv.at[k, core],
+            device_id=mate(k, c),
+            device_id_type=MESH,
+        )
+
+    def late_arrived(k, c):
+        pltpu.make_async_remote_copy(
+            src_ref=lates.at[k, c],
+            dst_ref=lates.at[k, c],
+            send_sem=late_send.at[k, c],
+            recv_sem=late_recv.at[k, c],
+            device_id=mate(k, c),
+            device_id_type=MESH,
+        ).wait_recv()
+
     ready(0)
     parts = combine(0)
     for part in range(2):
@@ -612,57 +643,35 @@
                 ring_copy(way, half - 1, part).wait_recv()
                 value = value + ring_in[way, half - 1, :, lanes].astype(F32)
         mid[:, lanes] = value.astype(BF16)
-
-    block = latent // groups
-    features = tokens_ref.shape[1]
-    column_rows = features // columns
-    ring_rows = column_rows // ring
-    last_rows = ring_rows // CORES
-
-    def late_lanes(k, c):
-        start = latent * (1 - c) + block * lax.rem(my_group + k, groups)
-        return pl.ds(pl.multiple_of(start, block), block)
-
-    def late_copy(k, c):
-        return pltpu.make_async_remote_copy(
-            src_ref=mid.at[:, late_lanes(k, c)],
-            dst_ref=lates.at[k, core],
-            send_sem=late_send.at[k, c],
-            recv_sem=late_recv.at[k, core],
-            device_id=mate(k, c),
-            device_id_type=MESH,
-        )
-
-    def late_arrived(k, c):
-        pltpu.make_async_remote_copy(
-            src_ref=lates.at[k, c],
-            dst_ref=lates.at[k, c],
-            send_sem=late_send.at[k, c],
-            recv_sem=late_recv.at[k, c],
-            device_id=mate(k, c),
-            device_id_type=MESH,
-        ).wait_recv()
-
-    for k, c in mates:
-        late_copy(k, c).start()
+        for k in range(1, groups):
+            late_copy(k, 1 - part).start()
+    late_copy(0, 1 - core).start()
     lates[0, core] = mid[:, late_lanes(0, core)]
-    mixed_ref[...] = dot(mid[:, 0:latent], up_ref[...], COLS)
-    token_grad_ref[...] = dot(mid[:, latent:], down_ref[...], COLS)
-    stores[0].start()
-    stores[1].start()
+
+    pair = CORES * tokens_here
+
+    def late_columns(k):
+        return lates[k].reshape(pair, block).astype(F32).T.astype(BF16)
 
     side_arrived(0, 1 - core)
-    if across > 1:
-        for c in range(CORES):
+    late_arrived(0, 1 - core)
+    term_sum[...] = dot(late_columns(0), sides[0].reshape(pair, features))
+    for k in near:
+        if k != across:
+            for c in range(CORES):
+                late_arrived(k, c)
+            term_sum[...] += dot(late_columns(k), sides[k].reshape(pair, features))
+    for c in range(CORES):
+        if across > 1:
             side_arrived(across, c)
-    for k, c in mates:
-        late_arrived(k, c)
-    both = groups * CORES * tokens_here
-    late_columns = lates[...].reshape(both, block).astype(F32).T.astype(BF16)
+        late_arrived(across, c)
+    last_columns = late_columns(across)
 
     def term_rows(k):
-        cols = pl.ds(pl.multiple_of(lax.rem(lax.div(me, ring * CORES) + k, columns) * column_rows, column_rows), column_rows)
-        return dot(late_columns, sides[:, :, :, cols].reshape(both, column_rows)).T
+        first = lax.rem(lax.div(me, ring * CORES) + k, columns) * column_rows
+        cols = pl.ds(pl.multiple_of(first, column_rows), column_rows)
+        term = dot(last_columns, sides[across, :, :, cols].reshape(pair, column_rows))
+        return (term_sum[:, cols] + term).T
 
     def x_copy(k):
         return pltpu.make_async_remote_copy(
@@ -678,6 +687,10 @@
         x_out[k] = term_rows(k).astype(BF16)
         x_copy(k).start()
     total = term_rows(0)
+    mixed_ref[...] = dot(mid[:, 0:latent], up_ref[...], COLS)
+    stores[0].start()
+    token_grad_ref[...] = dot(mid[:, latent:], down_ref[...], COLS)
+    stores[1].start()
     for k in near:
         grad_copy(k).wait_recv()
         gate_grad_ref[...] += grads_in[k, 0:latent, 0:share].astype(F32)
@@ -823,6 +836,7 @@
             pltpu.VMEM((count, 2 * latent), BF16),
             pltpu.VMEM((groups, CORES, count, features), BF16),
             pltpu.VMEM((groups, CORES, count, block), BF16),
+            pltpu.VMEM((block, features), F32),
             pltpu.VMEM((columns, features // columns, block), BF16),
             pltpu.VMEM((columns, features // columns, block), BF16),
             pltpu.VMEM((ring, ring_rows, block), F32),

time: 123 us -> 119 us (0.967)
  Pallas kernels: 115 us -> 112 us
    pallas_call x1, Pallas kernels: 115 us -> 112 us  [layer(): pl.pallas_call(partial(layer_kernel, ring), out_shape=results, in_specs=[...]
where the time goes in v5:
time: 119 us
  Pallas kernels  112 us (94%)
  local copies, waits for them, and re-layouts  3.98 us (3%)
  other arithmetic  3.09 us (3%)
    pallas_call x1, Pallas kernels, layer(): pl.pallas_call(partial(layer_kernel, ring), out_shape=results, in_specs=[...  112 us
    convert_element_type x2, other arithmetic, shards(): mixed, grad_tokens = (mixed.astype(BF16), grad_tokens.astype(BF16))  3.09 us
    unnamed x11, local copies, waits for them, and re-layouts  2.4 us

profile of v5, /device:TPU:1, one launch (start us, length us, event | category | flops | bytes accessed | tf_op | source)
XLA Modules:
  0.0 119.3 jit_solution(11868188460675367881)
XLA Ops:
  0.6 111.5 %layer.1 = (f32[128,2048]{1,0:T(8,128)}, f32[128,2048]{1,0:T(8,128)}, f32[2,32,512]{2,1,0:T(8,128)}, f32[512,256]{1,0:T(8,128)}, f32[512,256]{1,0:T(8,128)}, /*index=5*/f32[256,512]{1,0:T(8,128)}) custom-call(s32[8,128]{1,0:T(8,128)} %bitcast.18, f32[8,128]{1,0:T(8,128)} %bitcast.19, bf16[128,2048]{1,0:T(8,128)(2,1)} %tokens_hbm.1, ...), custom_call_target="tpu_custom_call" | custom-call | tf_op jit(solution)/shard_map/layer/pallas_call | solution.py:827
  112.2 0.0 copy-start
  112.2 0.0 copy-start.3
  112.2 0.0 copy-start.2
  112.2 2.2 %convert_element_type.6 = bf16[128,2048]{1,0:T(8,128)(2,1)} convert(f32[128,2048]{1,0:T(8,128)} %get-tuple-element.13) | non-fusion elementwise | flops 262144 | bytes 1572864 | tf_op jit(solution)/shard_map/convert_element_type | solution.py:918
  114.4 0.0 copy-start.1
  114.4 1.6 %slice_bitcast_fusion = (f32[32,512]{1,0:T(8,128)}, f32[32,512]{1,0:T(8,128)}) fusion(f32[2,32,512]{2,1,0:T(8,128)} %get-tuple-element.15), kind=kLoop, calls=%fused_computation | loop fusion | bytes 262144 | tf_op jit(solution)/shard_map/squeeze | solution.py:919
  116.0 0.0 copy-done
  116.0 0.9 convert_element_type.7
  116.9 0.0 copy-done.3
  116.9 0.8 copy.19
  117.7 0.0 copy-done.2
  117.7 0.8 copy.20
  118.5 0.0 copy-done.1
  118.5 0.8 copy.21
Async XLA Ops:
  112.2 3.9 %copy-start = (f32[128,2048]{1,0:T(8,128)S(1)}, f32[128,2048]{1,0:T(8,128)}, u32[]{:S(2)}) copy-start(f32[128,2048]{1,0:T(8,128)} %get-tuple-element.14) | copy-start | bytes 3145732
  112.2 4.7 %copy-start.3 = (f32[512,256]{1,0:T(8,128)S(1)}, f32[512,256]{1,0:T(8,128)}, u32[]{:S(2)}) copy-start(f32[512,256]{1,0:T(8,128)} %get-tuple-element.16) | copy-start | bytes 1572868
  112.2 5.5 %copy-start.2 = (f32[512,256]{1,0:T(8,128)S(1)}, f32[512,256]{1,0:T(8,128)}, u32[]{:S(2)}) copy-start(f32[512,256]{1,0:T(8,128)} %get-tuple-element.17) | copy-start | bytes 1572868
  114.4 4.0 %copy-start.1 = (f32[256,512]{1,0:T(8,128)S(1)}, f32[256,512]{1,0:T(8,128)}, u32[]{:S(2)}) copy-start(f32[256,512]{1,0:T(8,128)} %get-tuple-element.18) | copy-start | bytes 1572868

commit v6 on v5

--- a/solution.py
+++ b/solution.py
@@ -463,12 +463,6 @@
         dispatch(ring - 1, part)
     slots_arrived(last_set)
     expert(last_set)
-    for c in range(CORES):
-        for k in near:
-            side_arrived(k, c)
-    if across > 1:
-        for c in range(CORES):
-            relay_copy(c).start()
     slots_arrived(last_set + 1)
     for s in range(last_set):
         send_back(s, 0)
@@ -480,6 +474,13 @@
     for s in range(last_set):
         for n in range(1, SET):
             send_back(s, n)
+
+    for c in range(CORES):
+        for k in near:
+            side_arrived(k, c)
+    if across > 1:
+        for c in range(CORES):
+            relay_copy(c).start()
 
     share = hidden // groups
     all_rows = peers * sets * SET_ROWS

time: 119 us -> 131 us (1.10)
  Pallas kernels: 112 us -> 123 us
    pallas_call x1, Pallas kernels: 112 us -> 123 us  [layer(): pl.pallas_call(partial(layer_kernel, ring), out_shape=results, in_specs=[...]
where the time goes in v6:
time: 131 us
  Pallas kernels  123 us (94%)
  local copies, waits for them, and re-layouts  3.98 us (3%)
  other arithmetic  3.09 us (2%)
    pallas_call x1, Pallas kernels, layer(): pl.pallas_call(partial(layer_kernel, ring), out_shape=results, in_specs=[...  123 us
    convert_element_type x2, other arithmetic, shards(): mixed, grad_tokens = (mixed.astype(BF16), grad_tokens.astype(BF16))  3.09 us

profile of v6, /device:TPU:1, one launch (start us, length us, event | category | flops | bytes accessed | tf_op | source)
XLA Modules:
  0.0 130.9 jit_solution(3965916871668642317)
XLA Ops:
  0.6 123.1 %layer.1 = (f32[128,2048]{1,0:T(8,128)}, f32[128,2048]{1,0:T(8,128)}, f32[2,32,512]{2,1,0:T(8,128)}, f32[512,256]{1,0:T(8,128)}, f32[512,256]{1,0:T(8,128)}, /*index=5*/f32[256,512]{1,0:T(8,128)}) custom-call(s32[8,128]{1,0:T(8,128)} %bitcast.18, f32[8,128]{1,0:T(8,128)} %bitcast.19, bf16[128,2048]{1,0:T(8,128)(2,1)} %tokens_hbm.1, ...), custom_call_target="tpu_custom_call" | custom-call | tf_op jit(solution)/shard_map/layer/pallas_call | solution.py:828
  123.8 0.0 copy-start
  123.8 0.0 copy-start.3
  123.8 0.0 copy-start.2
  123.8 2.2 %convert_element_type.6 = bf16[128,2048]{1,0:T(8,128)(2,1)} convert(f32[128,2048]{1,0:T(8,128)} %get-tuple-element.13) | non-fusion elementwise | flops 262144 | bytes 1572864 | tf_op jit(solution)/shard_map/convert_element_type | solution.py:919
  126.0 0.0 copy-start.1
  126.0 1.6 %slice_bitcast_fusion = (f32[32,512]{1,0:T(8,128)}, f32[32,512]{1,0:T(8,128)}) fusion(f32[2,32,512]{2,1,0:T(8,128)} %get-tuple-element.15), kind=kLoop, calls=%fused_computation | loop fusion | bytes 262144 | tf_op jit(solution)/shard_map/squeeze | solution.py:920
  127.6 0.0 copy-done
  127.6 0.9 convert_element_type.7
  128.5 0.0 copy-done.3
  128.5 0.8 copy.19
  129.3 0.0 copy-done.2
  129.3 0.8 copy.20
  130.1 0.0 copy-done.1
  130.1 0.8 copy.21
Async XLA Ops:
  123.8 3.9 %copy-start = (f32[128,2048]{1,0:T(8,128)S(1)}, f32[128,2048]{1,0:T(8,128)}, u32[]{:S(2)}) copy-start(f32[128,2048]{1,0:T(8,128)} %get-tuple-element.14) | copy-start | bytes 3145732
  123.8 4.7 %copy-start.3 = (f32[512,256]{1,0:T(8,128)S(1)}, f32[512,256]{1,0:T(8,128)}, u32[]{:S(2)}) copy-start(f32[512,256]{1,0:T(8,128)} %get-tuple-element.16) | copy-start | bytes 1572868
  123.8 5.5 %copy-start.2 = (f32[512,256]{1,0:T(8,128)S(1)}, f32[512,256]{1,0:T(8,128)}, u32[]{:S(2)}) copy-start(f32[512,256]{1,0:T(8,128)} %get-tuple-element.17) | copy-start | bytes 1572868
  126.0 4.0 %copy-start.1 = (f32[256,512]{1,0:T(8,128)S(1)}, f32[256,512]{1,0:T(8,128)}, u32[]{:S(2)}) copy-start(f32[256,512]{1,0:T(8,128)} %get-tuple-element.18) | copy-start | bytes 1572868
